TPU v7x, 256 devices: a whole 4x4x8 slice. The times are simulated.
256 devices in a mesh: dir: 8 (over x, core), sx: 4 (over y), sy: 8 (over z).
Axes of the slice: x: 4, y: 4, z: 8, core: 2. Of those that a mesh axis runs over, the one named last changes fastest.
Arguments:
- signs_x: int32 [8, 256], P('dir', 'sx'), may hold values from -2147483648 to 2147483647, as said below
- signs_y: int32 [8, 1024], P('dir', 'sy'), may hold values from -2147483648 to 2147483647, as said below
- heights: int32 [256, 1024], P('sx', 'sy'), may hold values from 0 to 63
- velocity: float32 [256, 1024], P('sx', 'sy'), may hold values from 1 to 2
- background: float32 [8, 256, 1024], P('dir', 'sx', 'sy'), may hold values from -4 to 4
Outputs:
- basis: float32 [256, 256, 1024], P('dir', 'sx', 'sy')
- factor: float32 [256, 256], P('dir')
Inputs may be any that keep to these rules, and one draw needn't show every extreme that they name: `signs_x`: packed sign words, every bit pattern possible. `signs_y`: packed sign words, every bit pattern possible.
All inputs are finite; a program needn't handle non-finite values.
Results may differ from a plain program's by a relative error of at most 0.00027.
Values sent between devices are 32-bit elements; how exact they have to be, the bound alone decides.
No kernel may reach another device: no remote copies, remote signals or barrier semaphores. Data moves between devices by JAX's collectives and lax.ppermute only.
A program may use at most 64 MiB of HBM per device.

v0:
```python
import math

import jax
import jax.numpy as jnp
from jax import lax
from jax.sharding import PartitionSpec as P

PROBES = 32
LEVELS = 64


tau_step = 0.02


def with_halo(cells, sides, width):
    for axis, dim in sides:
        count = lax.axis_size(axis)
        ends = count - 1
        head = lax.slice_in_dim(cells, 0, width, axis=dim)
        tail = lax.slice_in_dim(cells, cells.shape[dim] - width, cells.shape[dim], axis=dim)
        cells = jnp.concatenate(
            [
                lax.ppermute(tail, axis, [(i, (i + 1) % count) for i in range(ends)]),
                cells,
                lax.ppermute(head, axis, [((i + 1) % count, i) for i in range(ends)]),
            ],
            axis=dim,
        )
    return cells


def from_partner(value, axis, distance):
    mask = 2**distance
    pairs = [(source, source ^ mask) for source in range(lax.axis_size(axis))]
    return lax.ppermute(value, axis, pairs)


def unpack_signs(packed, per_group):
    bit_index = jnp.arange(per_group, dtype=jnp.int32)
    bit_values = jnp.right_shift(packed[:, None, :], bit_index[None, :, None]) & 1
    signed = (2 * bit_values - 1).astype(jnp.float32)
    return signed.reshape(packed.shape[0] * per_group, packed.shape[1])


def apply_step(wavefield, stiffness):
    weighted = stiffness * wavefield
    padded = with_halo(weighted, (("sx", 1), ("sy", 2)), 1)
    laplace = (
        padded[:, 2:, 1:-1]
        + padded[:, :-2, 1:-1]
        + padded[:, 1:-1, 2:]
        + padded[:, 1:-1, :-2]
        - 4.0 * weighted
    )
    return wavefield + tau_step * stiffness * laplace


def responses_for(signs_first, signs_second, shot_data, stiffness):
    first_signs = unpack_signs(signs_first, PROBES)
    second = unpack_signs(signs_second, PROBES)
    kronecker = first_signs[:, :, None] * second[:, None, :]
    groups = shot_data.shape[0]
    rows_x = shot_data.shape[1]
    rows_y = shot_data.shape[2]
    rolled = jnp.roll(kronecker.reshape(groups, PROBES, rows_x, rows_y), -1, axis=1).reshape(
        kronecker.shape
    )
    probe_dirs = kronecker + 0.5 * rolled
    shot_fields = jnp.repeat(shot_data, PROBES, axis=0)
    wavefield = shot_fields * probe_dirs
    for repeat in range(4):
        wavefield = apply_step(wavefield, stiffness[None])
    return (shot_fields * wavefield).reshape(groups * PROBES, rows_x * rows_y)


def leaf_factor(response):
    local_gram = jnp.dot(
        response, response.T, precision=lax.Precision.HIGHEST, preferred_element_type=jnp.float32
    )
    gram_matrix = lax.psum(local_gram, ("sx", "sy"))
    factor_low = jnp.linalg.cholesky(gram_matrix)
    orthonormal = lax.linalg.triangular_solve(factor_low, response, left_side=True, lower=True)
    return (orthonormal, factor_low.T)


def merge_level(q_low, q_high, r_low, r_high):
    highest = lax.Precision.HIGHEST
    local_cross = jnp.einsum("pkc,pmc->pkm", q_low, q_high, precision=highest)
    cross_terms = lax.psum(local_cross, ("sx", "sy"))
    residue = q_high - jnp.einsum("pkm,pkc->pmc", cross_terms, q_low, precision=highest)
    local_remain = jnp.einsum("pmc,pnc->pmn", residue, residue, precision=highest)
    remain = lax.psum(local_remain, ("sx", "sy"))
    chol_low = jnp.linalg.cholesky(remain)
    fresh_rows = lax.linalg.triangular_solve(chol_low, residue, left_side=True, lower=True)
    merged_q = jnp.concatenate([q_low, fresh_rows], axis=1)
    upper_rows = jnp.concatenate(
        [r_low, jnp.einsum("pkm,pmn->pkn", cross_terms, r_high, precision=highest)], axis=2
    )
    bottom = jnp.concatenate(
        [jnp.zeros_like(r_low), jnp.einsum("pmk,pmn->pkn", chol_low, r_high, precision=highest)],
        axis=2,
    )
    merged_r = jnp.concatenate([upper_rows, bottom], axis=1)
    return (merged_q, merged_r)


def shards(signs_x, signs_y, heights, velocity, background):
    rows_x = background.shape[1]
    rows_y = background.shape[2]
    stiffness = velocity * jnp.sqrt(1.0 + heights.astype(jnp.float32) / LEVELS)
    groups = lax.axis_size("dir")
    count_levels = groups.bit_length() - 1
    response = responses_for(signs_x, signs_y, background, stiffness)
    orthonormal, factor_r = leaf_factor(response)
    for level_index in range(count_levels):
        partner_q, partner_r = from_partner((orthonormal, factor_r), "dir", level_index)
        is_upper = jnp.right_shift(lax.axis_index("dir"), level_index) & 1
        is_upper = is_upper == 1
        q_low = jnp.where(is_upper, partner_q, orthonormal)
        q_high = jnp.where(is_upper, orthonormal, partner_q)
        r_low = jnp.where(is_upper, partner_r, factor_r)
        r_high = jnp.where(is_upper, factor_r, partner_r)
        merged_q, merged_r = merge_level(q_low[None], q_high[None], r_low[None], r_high[None])
        orthonormal = merged_q[0]
        factor_r = merged_r[0]
    cell_count = math.sqrt(rows_x * rows_y * lax.axis_size("sx") * lax.axis_size("sy"))
    row_start = lax.axis_index("dir") * PROBES
    own_q = lax.dynamic_slice_in_dim(orthonormal, row_start, PROBES, 0)
    own_r = lax.dynamic_slice_in_dim(factor_r, row_start, PROBES, 0)
    basis = (own_q * cell_count).reshape(PROBES, rows_x, rows_y)
    factor = own_r / cell_count
    return (basis, factor)


def solution(mesh):
    in_specs = (P("dir", "sx"), P("dir", "sy"), P("sx", "sy"), P("sx", "sy"), P("dir", "sx", "sy"))
    out_specs = (P("dir", "sx", "sy"), P("dir", None))
    return jax.shard_map(shards, mesh=mesh, in_specs=in_specs, out_specs=out_specs, check_vma=False)
```

profile of v0, /device:TPU:1, one launch (start us, length us, event | category | flops | bytes accessed | tf_op | source)
XLA Modules:
  0.0 1281.2 jit_solution(17873428085590534502)
XLA Ops:
  10.9 4.7 collective-permute-start.1
  23.2 4.3 collective-permute-start.3
  36.6 4.3 collective-permute-start.5
  58.9 4.3 collective-permute-start.9
  67.2 4.4 collective-permute-start.11
  79.2 4.3 collective-permute-start.13
  89.7 5.4 collective-permute-start.15
  102.4 119.4 %psum.49 = f32[32,32]{0,1:T(8,128)S(1)} all-reduce(f32[32,32]{0,1:T(8,128)S(1)} %convolution_bitcast_fusion.12), channel_id=1, replica_groups=mesh['dir'=8,'sx'=4,'sy'=8] {'sx','sy'}, use_global_device_ids=true, to_apply=%region_0.1 | all-reduce | flops 1024 | bytes 8192 | tf_op jit(solution)/shard_map/psum | solution.py:80
  229.6 38.9 %collective-permute-start.16 = (f32[32,8192]{1,0:T(8,128)S(1)}, f32[32,8192]{1,0:T(8,128)S(1)}, u32[]{:S(2)}, u32[]{:S(2)}) collective-permute-start(f32[32,8192]{1,0:T(8,128)S(1)} %fusion.4), channel_id=1, source_target_pairs={{0,32},{32,0},{64,96},{96,64},{128,160},{160,128},{192,224},{224,1... | collective-permute-start | bytes 3145736 | tf_op jit(solution)/shard_map/ppermute | solution.py:35
  271.9 110.9 %psum.50 = f32[32,32]{1,0:T(8,128)S(1)} all-reduce(f32[32,32]{1,0:T(8,128)S(1)} %fusion.37), channel_id=1, replica_groups=mesh['dir'=8,'sx'=4,'sy'=8] {'sx','sy'}, use_global_device_ids=true, to_apply=%region_3.4 | all-reduce | flops 1024 | bytes 8192 | tf_op jit(solution)/shard_map/psum | solution.py:89
  384.9 110.1 %psum.51 = f32[1,32,32]{1,2,0:T(8,128)S(1)} all-reduce(f32[1,32,32]{1,2,0:T(8,128)S(1)} %convolution_bitcast_fusion.11), channel_id=1, replica_groups=mesh['dir'=8,'sx'=4,'sy'=8] {'sx','sy'}, use_global_device_ids=true, to_apply=%region_4.5 | all-reduce | flops 1024 | bytes 8192 | tf_op jit(solution)/shard_map/psum | solution.py:92
  505.6 24.0 %collective-permute-done.17 = f32[64,8192]{1,0:T(8,128)} collective-permute-done((f32[64,8192]{1,0:T(8,128)}, f32[64,8192]{1,0:T(8,128)}, u32[]{:S(2)}, u32[]{:S(2)}) %collective-permute-start.17) | collective-permute-done | bytes 2097184 | tf_op jit(solution)/shard_map/ppermute | solution.py:35
  533.1 110.5 %psum.52 = f32[64,64]{1,0:T(8,128)S(1)} all-reduce(f32[64,64]{1,0:T(8,128)S(1)} %fusion.35), channel_id=1, replica_groups=mesh['dir'=8,'sx'=4,'sy'=8] {'sx','sy'}, use_global_device_ids=true, to_apply=%region_7.8 | all-reduce | flops 4096 | bytes 32768 | tf_op jit(solution)/shard_map/psum | solution.py:89
  650.5 110.6 %psum.53 = f32[1,64,64]{1,2,0:T(8,128)S(1)} all-reduce(f32[1,64,64]{1,2,0:T(8,128)S(1)} %convolution_bitcast_fusion.8), channel_id=1, replica_groups=mesh['dir'=8,'sx'=4,'sy'=8] {'sx','sy'}, use_global_device_ids=true, to_apply=%region_8.9 | all-reduce | flops 4096 | bytes 32768 | tf_op jit(solution)/shard_map/psum | solution.py:92
  761.2 5.8 custom-call.30
  768.4 4.9 custom-call.31
  782.6 112.2 %collective-permute-start.19 = (f32[32,32]{0,1:T(8,128)S(1)}, f32[32,32]{0,1:T(8,128)S(1)}, u32[]{:S(2)}, u32[]{:S(2)}) collective-permute-start(f32[32,32]{0,1:T(8,128)S(1)} %get-tuple-element.34), channel_id=1, source_target_pairs={{0,32},{32,0},{64,96},{96,64},{128,160},{160,128},{192,224},{224,1... | collective-permute-start | bytes 12296 | tf_op jit(solution)/shard_map/ppermute | solution.py:35
  908.4 7.9 fusion
  920.5 167.3 %all-reduce.6.cloned.1.call-done = f32[128,128]{1,0:T(8,128)} async-done(((f32[128,128]{1,0:T(8,128)}), f32[128,128]{1,0:T(8,128)}) %all-reduce.6.cloned.1.call-update) | async-done | bytes 65552 | tf_op jit(solution)/shard_map/psum | solution.py:89
  1087.8 7.6 convolution_subtract_fusion
  1101.8 138.5 %all-reduce.8.cloned.1.call-done = f32[1,128,128]{1,2,0:T(8,128)} async-done(((f32[1,128,128]{1,2,0:T(8,128)}), f32[1,128,128]{1,2,0:T(8,128)}) %all-reduce.8.cloned.1.call-update) | async-done | bytes 65552 | tf_op jit(solution)/shard_map/psum | solution.py:92
  1242.1 11.9 custom-call.32
  1257.1 9.8 custom-call.33
  1266.9 5.6 convolution_bitcast_fusion
  (156 shorter events, 138.5 us)
Async XLA Ops:
  7.2 1080.7 %all-reduce.6.cloned.1.call-start = ((), (), s32[]{:S(2)}) async-start(), calls=%async_computation | async-start | bytes 131072 | tf_op jit(solution)/shard_map/psum | solution.py:89
  9.6 6.0 collective-permute-start
  10.9 5.5 collective-permute-start.1
  20.1 7.5 collective-permute-start.2
  23.2 6.3 collective-permute-start.3
  35.3 5.6 collective-permute-start.4
  36.6 5.1 collective-permute-start.5
  45.0 6.2 collective-permute-start.6
  47.0 5.3 collective-permute-start.7
  57.6 5.6 collective-permute-start.8
  58.9 5.1 collective-permute-start.9
  65.2 6.4 collective-permute-start.10
  67.2 5.5 collective-permute-start.11
  77.9 5.6 collective-permute-start.12
  79.2 5.1 collective-permute-start.13
  87.7 7.4 collective-permute-start.14
  89.7 7.3 collective-permute-start.15
  229.6 41.2 %collective-permute-start.16 = (f32[32,8192]{1,0:T(8,128)S(1)}, f32[32,8192]{1,0:T(8,128)S(1)}, u32[]{:S(2)}, u32[]{:S(2)}) collective-permute-start(f32[32,8192]{1,0:T(8,128)S(1)} %fusion.4), channel_id=1, source_target_pairs={{0,32},{32,0},{64,96},{96,64},{128,160},{160,128},{192,224},{224,1... | collective-permute-start | bytes 3145736 | tf_op jit(solution)/shard_map/ppermute | solution.py:35
  504.4 25.2 %collective-permute-start.17 = (f32[64,8192]{1,0:T(8,128)}, f32[64,8192]{1,0:T(8,128)}, u32[]{:S(2)}, u32[]{:S(2)}) collective-permute-start(f32[64,8192]{1,0:T(8,128)} %maximum_bitcast_fusion.1), channel_id=1, source_target_pairs={{0,64},{32,96},{64,0},{96,32},{128,192},{160,224},{192,128},{224,1... | collective-permute-start | bytes 6291464 | tf_op jit(solution)/shard_map/ppermute | solution.py:35
  779.8 128.6 %collective-permute-start.18 = (f32[128,8192]{1,0:T(8,128)}, f32[128,8192]{1,0:T(8,128)}, u32[]{:S(2)}, u32[]{:S(2)}) collective-permute-start(f32[128,8192]{1,0:T(8,128)} %maximum_bitcast_fusion), channel_id=1, source_target_pairs={{0,128},{32,160},{64,192},{96,224},{128,0},{160,32},{192,64},{224,... | collective-permute-start | bytes 12582920 | tf_op jit(solution)/shard_map/ppermute | solution.py:35
  782.6 113.1 %collective-permute-start.19 = (f32[32,32]{0,1:T(8,128)S(1)}, f32[32,32]{0,1:T(8,128)S(1)}, u32[]{:S(2)}, u32[]{:S(2)}) collective-permute-start(f32[32,32]{0,1:T(8,128)S(1)} %get-tuple-element.34), channel_id=1, source_target_pairs={{0,32},{32,0},{64,96},{96,64},{128,160},{160,128},{192,224},{224,1... | collective-permute-start | bytes 12296 | tf_op jit(solution)/shard_map/ppermute | solution.py:35
  896.7 4.7 collective-permute-start.20
  902.5 5.8 collective-permute-start.21
  916.3 324.0 %all-reduce.8.cloned.1.call-start = ((), (), s32[]{:S(2)}) async-start(), calls=%async_computation.1 | async-start | bytes 131072 | tf_op jit(solution)/shard_map/psum | solution.py:92
  (12 other events, 180.4 us)
Sparse Core Ops, SparseCore 0:
  916.4 171.3 all-reduce.5
  1101.6 138.6 all-reduce.7
where the time goes:
time: 1290 us; the launch traced here: 1280 us
  blocking collectives  562 us (44%)
  waiting for transfers between devices  343 us (27%)
  starting transfers between devices  206 us (16%)
  other arithmetic  74 us (6%)
  matrix products  47 us (4%)
  local copies, waits for them, and re-layouts  35.4 us (3%)
  between operations  15.2 us (1%)
    psum x2, blocking collectives, merge_level(): cross_terms = lax.psum(local_cross, ('sx', 'sy'))  221 us
    psum x2, blocking collectives, merge_level(): remain = lax.psum(local_remain, ('sx', 'sy'))  221 us
    psum x1, waiting for transfers between devices, merge_level(): cross_terms = lax.psum(local_cross, ('sx', 'sy'))  167 us
    ppermute x6, starting transfers between devices, from_partner(): return lax.ppermute(value, axis, pairs)  159 us
    psum x1, waiting for transfers between devices, merge_level(): remain = lax.psum(local_remain, ('sx', 'sy'))  139 us
    psum x1, blocking collectives, leaf_factor(): gram_matrix = lax.psum(local_gram, ('sx', 'sy'))  119 us
    ppermute x8, starting transfers between devices, with_halo(): lax.ppermute(tail, axis, [(i, (i + 1) % count) for i in range(ends)])  35.7 us
    ppermute x6, waiting for transfers between devices, from_partner(): return lax.ppermute(value, axis, pairs)  33.3 us
  transfers between devices with their start and end apart: 24, of which 11 were waited for; matrix products, arithmetic and copies ran while one was open for 1% of the time, Pallas kernels for 0%

commit v1 on v0

v1 whole, which is shorter than its diff:
```python
import functools
import math

import jax
import jax.numpy as jnp
from jax import lax
from jax.experimental import pallas as pl
from jax.experimental.pallas import tpu as pltpu
from jax.sharding import PartitionSpec as P

PROBES = 32
LEVELS = 64
HALO = 4
ROWS = 8
tau_step = 0.02

F32 = jnp.float32
BF16 = jnp.bfloat16
TN = (((0,), (0,)), ((), ()))
NT = (((1,), (1,)), ((), ()))


def split2(x):
    high = x.astype(BF16)
    return high, (x - high.astype(F32)).astype(BF16)


def split3(x):
    high = x.astype(BF16).astype(F32)
    rest = x - high
    mid = rest.astype(BF16).astype(F32)
    return high, mid, rest - mid


def response_kernel(shots, nx, ny, field_ref, stiff_ref, gram_ref, high_ref, low_ref,
                    first, first_next, second, second_next, coef, w0, w1, w2, w3, total):
    dirs = shots * PROBES
    ext_x, ext_y = nx + 2 * HALO, ny + 2 * HALO
    step = pl.program_id(0)

    @pl.when(step == 0)
    def _():
        total[...] = jnp.zeros_like(total)
        words = jnp.concatenate(
            [field_ref[g, ext_x:ext_x + 8, :] for g in range(shots)], axis=0
        ).astype(BF16)
        row = lax.broadcasted_iota(jnp.int32, (8 * shots, dirs), 0)
        col = lax.broadcasted_iota(jnp.int32, (8 * shots, dirs), 1)

        def bits(offset, shift):
            probe = (col + shift) % PROBES
            pick = (row // 8 == col // PROBES) & (row % 8 - offset == probe // 8)
            value = lax.dot_general(words, jnp.where(pick, 1.0, 0.0).astype(BF16), TN, preferred_element_type=F32)
            lane = (lax.broadcasted_iota(jnp.int32, value.shape, 1) + shift) % 8
            bit = jnp.right_shift(value.astype(jnp.int32), lane) & 1
            return (2 * bit - 1).astype(F32)

        first[...] = bits(0, 0)[:ext_x]
        first_next[...] = 0.5 * bits(0, 1)[:ext_x]
        second[...] = bits(4, 0)
        second_next[...] = bits(4, 1)

    row = lax.broadcasted_iota(jnp.int32, (32, dirs + 128), 0)
    col = lax.broadcasted_iota(jnp.int32, (32, dirs + 128), 1)
    in_shot = (row < 24) & (row % 8 == col // PROBES) & (col < dirs)
    in_coef = (row >= 24) & (row < 27) & (col >= dirs)
    expand = jnp.where(in_shot | in_coef, 1.0, 0.0).astype(BF16)
    sub = lax.broadcasted_iota(jnp.int32, (8, ext_y), 0)

    def stencil(src, row_at, dst):
        up, mid, down = (row_at - 1) & 3, row_at & 3, (row_at + 1) & 3
        c = coef[row_at & 7]
        out = []
        for h in range(dirs // 128):
            lanes = slice(128 * h, 128 * h + 128)
            w = src[mid, :, lanes]
            around = (src[up, :, lanes] + src[down, :, lanes]) + (
                pltpu.roll(w, 1, 0) + pltpu.roll(w, ext_y - 1, 0)
            )
            new = w + c * (around - 4.0 * w)
            if dst is not None:
                dst[mid, :, lanes] = new
            out.append(new)
        return out

    for k in range(ROWS):
        i = step * ROWS + k
        s_row = stiff_ref[pl.ds(i, 1), :]
        shot_rows = jnp.concatenate([field_ref[g, pl.ds(i, 1), :] for g in range(shots)], axis=0)
        c3 = split3(tau_step * s_row * s_row)
        c_rows = jnp.where(sub == 0, c3[0], jnp.where(sub == 1, c3[1], jnp.where(sub == 2, c3[2], 0.0)))
        lhs = jnp.concatenate([*split3(shot_rows * s_row), c_rows], axis=0).astype(BF16)
        wide = lax.dot_general(lhs, expand, TN, preferred_element_type=F32)
        coef[i & 7] = wide[:, dirs:]
        probe = first[pl.ds(i, 1), :] * second[...] + first_next[pl.ds(i, 1), :] * second_next[...]
        w0[i & 3] = wide[:, :dirs] * probe
        stencil(w0, i - 1, w1)
        stencil(w1, i - 2, w2)
        stencil(w2, i - 3, w3)
        last = stencil(w3, i - 4, None)
        at = jnp.maximum(i - HALO, 0)
        s_row = stiff_ref[pl.ds(at, 1), :]
        shot_rows = jnp.concatenate([field_ref[g, pl.ds(at, 1), :] for g in range(shots)], axis=0)
        scale = shot_rows / jnp.where(s_row > 0.0, s_row, 1.0)
        lhs = jnp.concatenate([*split3(scale), jnp.zeros_like(scale)], axis=0).astype(BF16)
        wide = lax.dot_general(lhs, expand[:, :dirs], TN, preferred_element_type=F32)
        for h in range(dirs // 128):
            lanes = slice(128 * h, 128 * h + 128)
            value = (last[h] * wide[:, lanes])[HALO:HALO + ny]
            high_ref[k, :, lanes], low_ref[k, :, lanes] = split2(value)

    @pl.when(step > 0)
    def _():
        high = high_ref[...].reshape(ROWS * ny, dirs)
        low = low_ref[...].reshape(ROWS * ny, dirs)
        total[:, :dirs] += lax.dot_general(high, high, TN, preferred_element_type=F32)
        total[:, dirs:] += lax.dot_general(high, low, TN, preferred_element_type=F32)

    @pl.when(step == pl.num_programs(0) - 1)
    def _():
        cross = total[:, dirs:]
        gram_ref[...] = total[:, :dirs] + cross + cross.T


def responses(fields, stiffness, shots, nx, ny):
    dirs = shots * PROBES
    ext_x, ext_y = nx + 2 * HALO, ny + 2 * HALO
    whole = lambda shape: pl.BlockSpec(shape, lambda s: (0,) * len(shape))
    block = pl.BlockSpec((ROWS, ny, dirs), lambda s: (jnp.maximum(s - 1, 0), 0, 0))
    return pl.pallas_call(
        functools.partial(response_kernel, shots, nx, ny),
        grid=(ext_x // ROWS,),
        in_specs=[whole(fields.shape), whole(stiffness.shape)],
        out_specs=[whole((dirs, dirs)), block, block],
        out_shape=[
            jax.ShapeDtypeStruct((dirs, dirs), F32),
            jax.ShapeDtypeStruct((nx, ny, dirs), BF16),
            jax.ShapeDtypeStruct((nx, ny, dirs), BF16),
        ],
        scratch_shapes=[
            pltpu.VMEM((ext_x, dirs), F32),
            pltpu.VMEM((ext_x, dirs), F32),
            pltpu.VMEM((ext_y, dirs), F32),
            pltpu.VMEM((ext_y, dirs), F32),
            pltpu.VMEM((8, ext_y, 128), F32),
            *[pltpu.VMEM((4, ext_y, dirs), F32) for _ in range(4)],
            pltpu.VMEM((dirs, 2 * dirs), F32),
        ],
        compiler_params=pltpu.CompilerParams(
            dimension_semantics=("arbitrary",), vmem_limit_bytes=48 * 2**20
        ),
        name="responses",
    )(fields, stiffness)


PANEL = 64
PIVOT = 4


def cholesky_kernel(n, scale, strip, index_ref, gram_ref, upper_ref, inverse_ref, table):
    tiles = n // 128
    groups = n // 8
    eye_row = lax.broadcasted_iota(jnp.int32, (8, 128), 0)
    eye_col = lax.broadcasted_iota(jnp.int32, (8, 128), 1)
    table[:, :n] = gram_ref[...]
    full = lambda x: jnp.broadcast_to(x, (8, 128))
    for panel in range(n // PANEL):
        start = panel * PANEL
        tile = start // 128
        live = [*range(tile, tiles), *range(tiles, tiles + tile + 1)]
        rows = {}
        for g in range(PANEL // 8):
            for t in live:
                at = start + 8 * g
                value = None
                if t < tiles or panel > 0:
                    value = table[at:at + 8, 128 * t:128 * t + 128] if (t < tiles or (t - tiles) * 128 < start) else None
                if t >= tiles:
                    unit = (eye_row + at == eye_col + 128 * (t - tiles)).astype(F32)
                    value = unit if value is None else value + unit
                rows[g, t] = value
        for micro in range(PANEL // PIVOT):
            k = micro * PIVOT
            gp, r = k // 8, k % 8
            lane = (start + k) % 128
            pivot_rows = [{t: full(rows[gp, t][r + j:r + j + 1, :]) for t in live} for j in range(PIVOT)]
            a = {
                (i, j): full(pivot_rows[i][tile][:, lane + j:lane + j + 1])
                for i in range(PIVOT) for j in range(i + 1)
            }
            low, inv = {}, []
            for j in range(PIVOT):
                d = a[j, j]
                for m in range(j):
                    d = d - low[j, m] * low[j, m]
                inv.append(lax.rsqrt(d))
                for i in range(j + 1, PIVOT):
                    v = a[i, j]
                    for m in range(j):
                        v = v - low[i, m] * low[j, m]
                    low[i, j] = v * inv[j]
            ready = []
            for j in range(PIVOT):
                out = {}
                for t in live:
                    v = pivot_rows[j][t]
                    for m in range(j):
                        v = v - low[j, m] * ready[m][t]
                    out[t] = v * inv[j]
                ready.append(out)
            for g in range(gp, PANEL // 8):
                if g == gp and r + PIVOT == 8:
                    pass
                else:
                    cols = []
                    for j in range(PIVOT):
                        v = full(rows[g, tile][:, lane + j:lane + j + 1])
                        for m in range(j):
                            v = v - cols[m] * low[j, m]
                        cols.append(v * inv[j])
                    if g == gp:
                        cols = [jnp.where(eye_row >= r + PIVOT, v, 0.0) for v in cols]
                    for t in live:
                        v = rows[g, t]
                        for j in range(PIVOT):
                            v = v - cols[j] * ready[j][t]
                        rows[g, t] = v
                if g == gp:
                    for t in live:
                        v = rows[g, t]
                        for j in range(PIVOT):
                            v = jnp.where(eye_row == r + j, ready[j][t], v)
                        rows[g, t] = v
        for g in range(PANEL // 8):
            for t in live:
                at = start + 8 * g
                value = rows[g, t]
                if t == tile:
                    value = jnp.where(eye_row + at <= eye_col + 128 * t, value, 0.0)
                table[at:at + 8, 128 * t:128 * t + 128] = value
            for t in range(tile):
                table[start + 8 * g:start + 8 * g + 8, 128 * t:128 * t + 128] = jnp.zeros((8, 128), F32)
            for t in range(tiles + tile + 1, 2 * tiles):
                table[start + 8 * g:start + 8 * g + 8, 128 * t:128 * t + 128] = jnp.zeros((8, 128), F32)
        below = start + PANEL
        if below < n:
            keep = below // 128
            for t in range(keep, tiles + tile + 1):
                if t == keep:
                    lo = 128 * keep
                    left = table[start:below, lo:n]
                    p3 = [v.astype(BF16) for v in split3(left)]
                    lhs = jnp.concatenate([p3[0], p3[0], p3[1], p3[0], p3[2], p3[1]], axis=0)
                lanes = slice(128 * t, 128 * t + 128)
                right = [v.astype(BF16) for v in split3(table[start:below, lanes])]
                rhs = jnp.concatenate([right[0], right[1], right[0], right[2], right[0], right[1]], axis=0)
                update = lax.dot_general(lhs, rhs, TN, preferred_element_type=F32)[below - lo:]
                if t < tiles or 128 * (t - tiles) < start:
                    table[below:, lanes] = table[below:, lanes] - update
                else:
                    table[below:, lanes] = -update
    own = pl.ds(pl.multiple_of(index_ref[0] * strip, strip), strip)
    upper_ref[...] = table[own, :n] * (1.0 / scale)
    inverse_ref[...] = table[own, n:] * scale


def factorise(gram, index, scale, strip):
    n = gram.shape[0]
    return pl.pallas_call(
        functools.partial(cholesky_kernel, n, scale, strip),
        in_specs=[pl.BlockSpec(memory_space=pltpu.SMEM), pl.BlockSpec(memory_space=pltpu.VMEM)],
        out_specs=[pl.BlockSpec(memory_space=pltpu.VMEM)] * 2,
        out_shape=[jax.ShapeDtypeStruct((strip, n), F32)] * 2,
        scratch_shapes=[pltpu.VMEM((n, 2 * n), F32)],
        compiler_params=pltpu.CompilerParams(vmem_limit_bytes=32 * 2**20),
        name="factorise",
    )(index, gram)


def basis_kernel(inverse_ref, high_ref, low_ref, out_ref):
    strip = inverse_ref.shape[0]
    high, low = split2(inverse_ref[...])
    both = jnp.concatenate([high, low], axis=0)
    for i in range(high_ref.shape[0]):
        main = lax.dot_general(both, high_ref[i], NT, preferred_element_type=F32)
        rest = lax.dot_general(high, low_ref[i], NT, preferred_element_type=F32)
        out_ref[:, i, :] = main[:strip] + (main[strip:] + rest)


def project(inverse, high, low):
    nx, ny, dirs = high.shape
    strip = inverse.shape[0]
    block = pl.BlockSpec((ROWS, ny, dirs), lambda s: (s, 0, 0))
    return pl.pallas_call(
        basis_kernel,
        grid=(nx // ROWS,),
        in_specs=[pl.BlockSpec(inverse.shape, lambda s: (0, 0)), block, block],
        out_specs=pl.BlockSpec((strip, ROWS, ny), lambda s: (0, s, 0)),
        out_shape=jax.ShapeDtypeStruct((strip, nx, ny), F32),
        compiler_params=pltpu.CompilerParams(
            dimension_semantics=("arbitrary",), vmem_limit_bytes=32 * 2**20
        ),
        name="project",
    )(inverse, high, low)


def edges(value, axis, dim):
    count = lax.axis_size(axis)
    size = value.shape[dim]
    head = lax.slice_in_dim(value, 0, HALO, axis=dim)
    tail = lax.slice_in_dim(value, size - HALO, size, axis=dim)
    before = lax.ppermute(tail, axis, [(i, i + 1) for i in range(count - 1)])
    after = lax.ppermute(head, axis, [(i + 1, i) for i in range(count - 1)])
    return jnp.concatenate([before, value, after], axis=dim)


def as_bytes(words):
    shifts = 8 * jnp.arange(4, dtype=jnp.int32)
    return (jnp.right_shift(words[None, :], shifts[:, None]) & 255).astype(F32)


def shards(signs_x, signs_y, heights, velocity, background):
    shots = lax.axis_size("dir")
    nx, ny = background.shape[1:]
    ext_x, ext_y = nx + 2 * HALO, ny + 2 * HALO
    stiffness = velocity * jnp.sqrt(1.0 + heights.astype(F32) / LEVELS)
    bytes_x = jnp.pad(as_bytes(signs_x[0]).T, ((0, 0), (0, ny - 4)))
    packed = edges(jnp.stack([background[0], stiffness, bytes_x]), "sx", 1)
    bytes_x = packed[2, :, :4].T
    packed = jnp.concatenate([packed[:2].reshape(2 * ext_x, ny), as_bytes(signs_y[0])], axis=0)
    packed = edges(packed, "sy", 1)
    stiffness = packed[ext_x:2 * ext_x]
    own = jnp.concatenate(
        [packed[:ext_x], jnp.pad(bytes_x, ((0, 0), (0, ext_y - ext_x))), packed[2 * ext_x:]], axis=0
    )
    fields = lax.all_to_all(jnp.broadcast_to(own[None], (shots, *own.shape)), "dir", 0, 0)
    gram, high, low = responses(fields, stiffness, shots, nx, ny)
    dirs = shots * PROBES
    index = lax.axis_index("dir")
    strip = lax.dynamic_slice_in_dim(gram, index * PROBES, PROBES, 0)
    terms = lax.all_to_all(strip.reshape(PROBES, dirs // 128, 128), ("sx", "sy"), 0, 0)
    row = jnp.sum(terms, axis=0, keepdims=True)
    gram = lax.all_to_all(jnp.broadcast_to(row, (dirs, *row.shape[1:])), ("dir", "sx", "sy"), 0, 0)
    gram = gram.reshape(dirs, dirs)
    scale = math.sqrt(nx * ny * lax.axis_size("sx") * lax.axis_size("sy"))
    factor, inverse = factorise(gram, index.reshape(1), scale, PROBES)
    return project(inverse, high, low), factor


def solution(mesh):
    in_specs = (P("dir", "sx"), P("dir", "sy"), P("sx", "sy"), P("sx", "sy"), P("dir", "sx", "sy"))
    out_specs = (P("dir", "sx", "sy"), P("dir", None))
    return jax.shard_map(shards, mesh=mesh, in_specs=in_specs, out_specs=out_specs, check_vma=False)
```

time: 1290 us -> 146 us (0.11)
  blocking collectives: 562 us -> 42.2 us
  waiting for transfers between devices: 343 us -> 19 us
  starting transfers between devices: 206 us -> 17.6 us
  other arithmetic: 74 us -> 2.95 us
  Pallas kernels: 0 us -> 52.9 us
  matrix products: 47 us -> 0 us
  local copies, waits for them, and re-layouts: 35.4 us -> 9.71 us
  between operations: 15.2 us -> 0.79 us
    psum x5 -> x0, blocking collectives: 562 us -> none  [the longest x2 221 us: merge_level(): cross_terms = lax.psum(local_cross, ('sx', 'sy'))]
    psum x2 -> x0, waiting for transfers between devices: 306 us -> none  [the longest x1 167 us: merge_level(): cross_terms = lax.psum(local_cross, ('sx', 'sy'))]
    ppermute x22 -> x4, starting transfers between devices: 205 us -> 10.2 us  [the longest x2 7.59 us: edges(): before = lax.ppermute(tail, axis, [(i, i + 1) for i in range(count - 1)])]
    pallas_call x0 -> x3, Pallas kernels: none -> 52.9 us  [the longest x1 35.9 us: responses(): pl.pallas_call(functools.partial(response_kernel, shots, nx, ny), grid=(e...]
    another operation x19 -> x2, other arithmetic: 47.8 us -> 0.05 us  [shards(): packed = edges(jnp.stack([background[0], stiffness, bytes_x]), 'sx', 1)]
    all_to_all x0 -> x2, blocking collectives: none -> 42.2 us  [the longest x1 22.8 us: shards(): lax.all_to_all(jnp.broadcast_to(row, (dirs, *row.shape[1:])), ('dir', 'sx...]
    dot_general x16 -> x0, matrix products: 35.7 us -> none  [the longest x3 12.5 us: merge_level(): jnp.einsum('pkm,pkc->pmc', cross_terms, q_low, precision=highest)]
    ppermute x22 -> x4, waiting for transfers between devices: 36.7 us -> 9.26 us  [the longest x2 7.7 us: edges(): after = lax.ppermute(head, axis, [(i + 1, i) for i in range(count - 1)])]
  transfers between devices with their start and end apart: 24 -> 5, of which waited for: 11 -> 4; matrix products, arithmetic and copies ran while one was open for 1% -> 1% of each run, Pallas kernels for 0% -> 0%
where the time goes in v1:
time: 146 us; the launch traced here: 145 us
  Pallas kernels  52.9 us (36%)
  blocking collectives  42.2 us (29%)
  waiting for transfers between devices  19 us (13%)
  starting transfers between devices  17.6 us (12%)
  local copies, waits for them, and re-layouts  9.71 us (7%)
  other arithmetic  2.95 us (2%)
    pallas_call x1, Pallas kernels, responses(): pl.pallas_call(functools.partial(response_kernel, shots, nx, ny), grid=(e...  35.9 us
    all_to_all x1, blocking collectives, shards(): lax.all_to_all(jnp.broadcast_to(row, (dirs, *row.shape[1:])), ('dir', 'sx...  22.8 us
    all_to_all x1, blocking collectives, shards(): lax.all_to_all(strip.reshape(PROBES, dirs // 128, 128), ('sx', 'sy'), 0, 0)  19.3 us
    pallas_call x1, Pallas kernels, factorise(): pl.pallas_call(functools.partial(cholesky_kernel, n, scale, strip), in_sp...  12.1 us
    all_to_all x1, waiting for transfers between devices, shards(): lax.all_to_all(jnp.broadcast_to(own[None], (shots, *own.shape)), 'dir', 0...  9.73 us
    unnamed x9, local copies, waits for them, and re-layouts  8.06 us
    ppermute x2, waiting for transfers between devices, edges(): after = lax.ppermute(head, axis, [(i + 1, i) for i in range(count - 1)])  7.7 us
    ppermute x2, starting transfers between devices, edges(): before = lax.ppermute(tail, axis, [(i, i + 1) for i in range(count - 1)])  7.59 us
  transfers between devices with their start and end apart: 5, of which 4 were waited for; matrix products, arithmetic and copies ran while one was open for 1% of the time, Pallas kernels for 0%

profile of v1, /device:TPU:1, one launch (start us, length us, event | category | flops | bytes accessed | tf_op | source)
XLA Modules:
  0.0 145.1 jit_solution(14822978962140754188)
XLA Ops:
  0.6 0.8 convert_element_type.14
  1.5 0.9 copy.22
  2.4 0.9 copy.21
  3.2 0.7 and_convert_fusion.1
  4.1 4.0 %collective-permute-start = (f32[3,4,128]{1,2,0:T(8,128)S(1)}, f32[3,4,128]{1,2,0:T(8,128)S(1)}, u32[]{:S(2)}, u32[]{:S(2)}) collective-permute-start(f32[3,4,128]{1,2,0:T(8,128)S(1)} %get-tuple-element.12), channel_id=1, source_target_pairs={{0,8},{8,16},{16,24},{1,9},{9,17},{17,25},{2,10},{10,18},{18,26},{... | collective-permute-start | bytes 18440 | tf_op jit(solution)/shard_map/ppermute | solution.py:312
  8.2 1.3 collective-permute-start.1
  9.5 0.7 and_convert_fusion
  10.2 1.5 %collective-permute-done = f32[3,4,128]{1,2,0:T(8,128)S(1)} collective-permute-done((f32[3,4,128]{1,2,0:T(8,128)S(1)}, f32[3,4,128]{1,2,0:T(8,128)S(1)}, u32[]{:S(2)}, u32[]{:S(2)}) %collective-permute-start) | collective-permute-done | bytes 6176 | tf_op jit(solution)/shard_map/ppermute | solution.py:312
  11.7 3.8 %collective-permute-done.1 = f32[3,4,128]{1,2,0:T(8,128)S(1)} collective-permute-done((f32[3,4,128]{1,2,0:T(8,128)S(1)}, f32[3,4,128]{1,2,0:T(8,128)S(1)}, u32[]{:S(2)}, u32[]{:S(2)}) %collective-permute-start.1) | collective-permute-done | bytes 6176 | tf_op jit(solution)/shard_map/ppermute | solution.py:313
  15.9 3.5 %collective-permute-start.2 = (f32[148,4]{1,0:T(8,128)S(1)}, f32[148,4]{1,0:T(8,128)S(1)}, u32[]{:S(2)}, u32[]{:S(2)}) collective-permute-start(f32[148,4]{1,0:T(8,128)S(1)} %get-tuple-element.14), channel_id=1, source_target_pairs={{0,1},{1,2},{2,3},{3,4},{4,5},{5,6},{6,7},{8,9},{9,10},{10,11},{11... | collective-permute-start | bytes 7112 | tf_op jit(solution)/shard_map/ppermute | solution.py:312
  19.4 1.3 collective-permute-start.3
  20.9 3.9 %collective-permute-done.3 = f32[148,4]{1,0:T(8,128)S(1)} collective-permute-done((f32[148,4]{1,0:T(8,128)S(1)}, f32[148,4]{1,0:T(8,128)S(1)}, u32[]{:S(2)}, u32[]{:S(2)}) %collective-permute-start.3) | collective-permute-done | bytes 2400 | tf_op jit(solution)/shard_map/ppermute | solution.py:313
  25.1 0.8 broadcast_in_dim.4
  25.9 7.4 %all-to-all-start = ((f32[8,80,136]{1,2,0:T(8,128)}), f32[8,80,136]{1,2,0:T(8,128)S(1)}, u32[]{:S(2)}, u32[]{:S(2)}) async-start(f32[8,80,136]{1,2,0:T(8,128)} %broadcast_in_dim.4), calls=%async_computation | async-start | bytes 1114112 | tf_op jit(solution)/shard_map/all_to_all | solution.py:336
  33.5 9.7 %all-to-all-done = f32[8,80,136]{1,2,0:T(8,128)S(1)} async-done(((f32[8,80,136]{1,2,0:T(8,128)}), f32[8,80,136]{1,2,0:T(8,128)S(1)}, u32[]{:S(2)}, u32[]{:S(2)}) %all-to-all-start) | async-done | bytes 348192 | tf_op jit(solution)/shard_map/all_to_all | solution.py:336
  43.2 0.3 copy.25.field_ref
  43.5 35.9 %responses.1 = (f32[256,256]{1,0:T(8,128)S(1)}, bf16[64,128,256]{2,1,0:T(8,128)(2,1)S(1)}, bf16[64,128,256]{2,1,0:T(8,128)(2,1)}) custom-call(f32[8,80,136]{2,1,0:T(8,128)S(1)} %copy.25.field_ref, f32[72,136]{1,0:T(8,128)S(1)} %pad_maximum_fusion.4.stiff_ref), custom_call_target="tpu_custom_call" | custom-call | tf_op jit(solution)/shard_map/responses/pallas_call | solution.py:130
  79.4 2.0 %copy-done = bf16[64,128,256]{2,1,0:T(8,128)(2,1)} copy-done((bf16[64,128,256]{2,1,0:T(8,128)(2,1)}, bf16[64,128,256]{2,1,0:T(8,128)(2,1)S(1)}, u32[]{:S(2)}) %copy-start) | copy-done | bytes 4194328
  81.4 19.3 %all_to_all.15 = f32[32,2,128]{2,1,0:T(2,128)S(1)} all-to-all(f32[32,2,128]{2,1,0:T(2,128)S(1)} %reshape.24), channel_id=1, replica_groups=mesh['dir'=8,'sx'=4,'sy'=8] {'sx','sy'}, dimensions={0} | all-to-all | bytes 65536 | tf_op jit(solution)/shard_map/all_to_all | solution.py:341
  100.9 22.8 %all_to_all.16 = f32[256,2,128]{2,1,0:T(2,128)S(1)} all-to-all(f32[256,2,128]{2,1,0:T(2,128)S(1)} %broadcast_in_dim.5), channel_id=1, replica_groups=mesh['dir'=8,'sx'=4,'sy'=8] {'dir','sx','sy'}, dimensions={0} | all-to-all | bytes 524288 | tf_op jit(solution)/shard_map/all_to_all | solution.py:343
  123.7 12.1 %factorise.1 = (f32[32,256]{1,0:T(8,128)}, f32[32,256]{1,0:T(8,128)S(1)}) custom-call(s32[1]{0:T(128)} %bitcast.index_ref, f32[256,256]{1,0:T(8,128)S(1)} %bitcast.16), custom_call_target="tpu_custom_call" | custom-call | tf_op jit(solution)/shard_map/factorise/pallas_call | solution.py:269
  135.8 2.2 %copy-done.1 = bf16[64,128,256]{2,1,0:T(8,128)(2,1)S(1)} copy-done((bf16[64,128,256]{2,1,0:T(8,128)(2,1)S(1)}, bf16[64,128,256]{2,1,0:T(8,128)(2,1)}, u32[]{:S(2)}) %copy-start.1) | copy-done | bytes 4194328
  138.0 2.2 %copy-done.2 = bf16[64,128,256]{2,1,0:T(8,128)(2,1)S(1)} copy-done((bf16[64,128,256]{2,1,0:T(8,128)(2,1)S(1)}, bf16[64,128,256]{2,1,0:T(8,128)(2,1)}, u32[]{:S(2)}) %copy-start.2) | copy-done | bytes 4194328
  140.2 5.0 %project.1 = f32[32,64,128]{2,1,0:T(8,128)} custom-call(f32[32,256]{1,0:T(8,128)S(1)} %get-tuple-element.8.inverse_ref, bf16[64,128,256]{2,1,0:T(8,128)(2,1)S(1)} %copy-done.1, bf16[64,128,256]{2,1,0:T(8,128)(2,1)S(1)} %copy-done.2), custom_call_target="tpu_custom_call" | custom-call | tf_op jit(solution)/shard_map/project/pallas_call | solution.py:294
  (24 shorter events, 1.3 us)
Async XLA Ops:
  4.1 7.6 %collective-permute-start = (f32[3,4,128]{1,2,0:T(8,128)S(1)}, f32[3,4,128]{1,2,0:T(8,128)S(1)}, u32[]{:S(2)}, u32[]{:S(2)}) collective-permute-start(f32[3,4,128]{1,2,0:T(8,128)S(1)} %get-tuple-element.12), channel_id=1, source_target_pairs={{0,8},{8,16},{16,24},{1,9},{9,17},{17,25},{2,10},{10,18},{18,26},{... | collective-permute-start | bytes 18440 | tf_op jit(solution)/shard_map/ppermute | solution.py:312
  8.2 7.3 %collective-permute-start.1 = (f32[3,4,128]{1,2,0:T(8,128)S(1)}, f32[3,4,128]{1,2,0:T(8,128)S(1)}, u32[]{:S(2)}, u32[]{:S(2)}) collective-permute-start(f32[3,4,128]{1,2,0:T(8,128)S(1)} %get-tuple-element.13), channel_id=1, source_target_pairs={{8,0},{16,8},{24,16},{9,1},{17,9},{25,17},{10,2},{18,10},{26,18},{... | collective-permute-start | bytes 18440 | tf_op jit(solution)/shard_map/ppermute | solution.py:313
  15.9 5.0 %collective-permute-start.2 = (f32[148,4]{1,0:T(8,128)S(1)}, f32[148,4]{1,0:T(8,128)S(1)}, u32[]{:S(2)}, u32[]{:S(2)}) collective-permute-start(f32[148,4]{1,0:T(8,128)S(1)} %get-tuple-element.14), channel_id=1, source_target_pairs={{0,1},{1,2},{2,3},{3,4},{4,5},{5,6},{6,7},{8,9},{9,10},{10,11},{11... | collective-permute-start | bytes 7112 | tf_op jit(solution)/shard_map/ppermute | solution.py:312
  19.4 5.3 %collective-permute-start.3 = (f32[148,4]{1,0:T(8,128)S(1)}, f32[148,4]{1,0:T(8,128)S(1)}, u32[]{:S(2)}, u32[]{:S(2)}) collective-permute-start(f32[148,4]{1,0:T(8,128)S(1)} %get-tuple-element.15), channel_id=1, source_target_pairs={{1,0},{2,1},{3,2},{4,3},{5,4},{6,5},{7,6},{9,8},{10,9},{11,10},{12... | collective-permute-start | bytes 7112 | tf_op jit(solution)/shard_map/ppermute | solution.py:313
  25.9 17.2 %all-to-all-start = ((f32[8,80,136]{1,2,0:T(8,128)}), f32[8,80,136]{1,2,0:T(8,128)S(1)}, u32[]{:S(2)}, u32[]{:S(2)}) async-start(f32[8,80,136]{1,2,0:T(8,128)} %broadcast_in_dim.4), calls=%async_computation | async-start | bytes 1114112 | tf_op jit(solution)/shard_map/all_to_all | solution.py:336
  79.4 2.0 %copy-start = (bf16[64,128,256]{2,1,0:T(8,128)(2,1)}, bf16[64,128,256]{2,1,0:T(8,128)(2,1)S(1)}, u32[]{:S(2)}) copy-start(bf16[64,128,256]{2,1,0:T(8,128)(2,1)S(1)} %get-tuple-element.9.high_ref) | copy-start | bytes 12582916
  135.8 2.2 %copy-start.1 = (bf16[64,128,256]{2,1,0:T(8,128)(2,1)S(1)}, bf16[64,128,256]{2,1,0:T(8,128)(2,1)}, u32[]{:S(2)}) copy-start(bf16[64,128,256]{2,1,0:T(8,128)(2,1)} %copy-done) | copy-start | bytes 12582916
  138.0 2.2 %copy-start.2 = (bf16[64,128,256]{2,1,0:T(8,128)(2,1)S(1)}, bf16[64,128,256]{2,1,0:T(8,128)(2,1)}, u32[]{:S(2)}) copy-start(bf16[64,128,256]{2,1,0:T(8,128)(2,1)} %get-tuple-element.10.low_ref) | copy-start | bytes 12582916

commit v2 on v1

v2 whole, which is shorter than its diff:
```python
import functools
import math

import jax
import jax.numpy as jnp
from jax import lax
from jax.experimental import pallas as pl
from jax.experimental.pallas import tpu as pltpu
from jax.sharding import PartitionSpec as P

PROBES = 32
LEVELS = 64
HALO = 4
ROWS = 8
tau_step = 0.02

F32 = jnp.float32
BF16 = jnp.bfloat16
TN = (((0,), (0,)), ((), ()))
NT = (((1,), (1,)), ((), ()))
VMEM = pl.BlockSpec(memory_space=pltpu.VMEM)
SMEM = pl.BlockSpec(memory_space=pltpu.SMEM)
HBM = pl.BlockSpec(memory_space=pltpu.HBM)


def split2(x):
    high = x.astype(BF16)
    return high, (x - high.astype(F32)).astype(BF16)


def split3(x):
    high = x.astype(BF16).astype(F32)
    rest = x - high
    mid = rest.astype(BF16).astype(F32)
    return high, mid, rest - mid


def sign_bytes(words):
    shape = (8, words.shape[1])
    shift = 8 * (lax.broadcasted_iota(jnp.int32, shape, 0) & 3)
    return (jnp.right_shift(jnp.broadcast_to(words, shape), shift) & 255).astype(F32)


def pack_x_kernel(signs_ref, heights_ref, velocity_ref, field_ref, stiff_ref, first_ref, last_ref):
    nx, ny = velocity_ref.shape
    stiff = velocity_ref[...] * jnp.sqrt(1.0 + heights_ref[...].astype(F32) / LEVELS)
    stiff_ref[...] = stiff
    octets = sign_bytes(signs_ref[...])
    for ref, start in ((first_ref, 0), (last_ref, nx - HALO)):
        ref[0:HALO, :] = field_ref[0, start:start + HALO, :]
        ref[HALO:2 * HALO, :] = stiff[start:start + HALO]
        ref[8:16, :] = jnp.zeros((8, ny), F32)
        ref[8:16, :nx] = octets


def pack_y_kernel(signs_ref, field_ref, stiff_ref, own_ref, above_ref, below_ref,
                  field_out, stiff_out, octets_out, first_ref, last_ref):
    nx, ny = stiff_ref.shape
    ext_x = nx + 2 * HALO
    field_out[0:HALO, :] = above_ref[0:HALO, :]
    field_out[HALO:HALO + nx, :] = field_ref[0]
    field_out[HALO + nx:ext_x, :] = below_ref[0:HALO, :]
    stiff_out[0:HALO, :] = above_ref[HALO:2 * HALO, :]
    stiff_out[HALO:HALO + nx, :] = stiff_ref[...]
    stiff_out[HALO + nx:ext_x, :] = below_ref[HALO:2 * HALO, :]
    lane = lax.broadcasted_iota(jnp.int32, (8, ny), 1)
    after = pltpu.roll(below_ref[8:16, :], nx + HALO, 1)
    before = pltpu.roll(above_ref[8:16, :], ny - nx + HALO, 1)
    own = pltpu.roll(own_ref[8:16, :], HALO, 1)
    octets_out[...] = jnp.where(lane < HALO, before, jnp.where(lane < HALO + nx, own, after))
    octets = sign_bytes(signs_ref[...])
    field, stiff = field_out[...], stiff_out[...]
    lane = lax.broadcasted_iota(jnp.int32, field.shape, 1)
    first_ref[0:ext_x, :] = jnp.where(lane < HALO, field, pltpu.roll(stiff, HALO, 1))
    first_ref[ext_x:, :] = octets
    last_ref[0:ext_x, :] = jnp.where(lane < 2 * HALO, pltpu.roll(field, 2 * HALO, 1), pltpu.roll(stiff, 3 * HALO, 1))
    last_ref[ext_x:, :] = octets


def pack_dir_kernel(index_ref, field_ref, stiff_ref, octets_ref, own_ref, left_ref, right_ref, send_ref, stiff_out):
    ext_x, ny = field_ref.shape
    half = (ext_x - 2 * HALO) // 2
    take = half + 2 * HALO
    left, right = left_ref[0:ext_x, :], right_ref[0:ext_x, :]
    lane = lax.broadcasted_iota(jnp.int32, left.shape, 1)
    field_side = jnp.where(lane < HALO, right, left)
    shift = lambda v: pltpu.roll(v, ny - HALO, 1)
    stiff_side = jnp.where(lane < HALO, shift(right), shift(left))
    lane = lax.broadcasted_iota(jnp.int32, (8, ny), 1)
    octet_side = jnp.where(lane < HALO, right_ref[ext_x:, :], pltpu.roll(left_ref[ext_x:, :], 2 * HALO, 1))
    own_octets = own_ref[ext_x:, :]
    for dest in range(send_ref.shape[0]):
        part = dest & 1
        rows = slice(part * half, part * half + take)
        send_ref[dest, 0:take, 0:ny] = field_ref[rows, :]
        send_ref[dest, 0:take, ny:] = field_side[rows, :2 * HALO]
        x_octets = octets_ref[...] if part == 0 else pltpu.roll(octets_ref[...], ny - half, 1)
        send_ref[dest, take:take + 4, 0:ny] = x_octets[0:4]
        send_ref[dest, take:take + 4, ny:] = jnp.zeros((4, 2 * HALO), F32)
        send_ref[dest, take + 4:take + 8, 0:ny] = own_octets[0:4]
        send_ref[dest, take + 4:take + 8, ny:] = octet_side[0:4, :2 * HALO]
    row = pl.multiple_of((index_ref[0] & 1) * half, half)
    stiff_out[:, 0:ny] = stiff_ref[pl.ds(row, take), :]
    spare = jnp.where(index_ref[0] & 1 == 1, stiff_side[half:half + take], stiff_side[0:take])
    stiff_out[:, ny:] = spare[:, :2 * HALO]


def small(kernel, shapes, specs, name):
    return pl.pallas_call(
        kernel,
        in_specs=specs,
        out_specs=[VMEM] * len(shapes),
        out_shape=[jax.ShapeDtypeStruct(shape, F32) for shape in shapes],
        name=name,
    )


def exchange(first, last, axis):
    count = lax.axis_size(axis)
    before = lax.ppermute(last, axis, [(i, i + 1) for i in range(count - 1)])
    after = lax.ppermute(first, axis, [(i + 1, i) for i in range(count - 1)])
    return before, after


PART = 32


def response_kernel(shots, nx, ny, index_ref, field_ref, stiff_ref, own_ref, other_ref, high_ref, low_ref,
                    expand, stack, spread, first, first_next, second, second_next,
                    coef, back, field, w0, w1, w2, w3, fold, total):
    dirs = shots * PROBES
    halves = dirs // 128
    ext_x, ext_y = nx + 2 * HALO, ny + 2 * HALO
    depth = ext_y // 8
    width = dirs + 256
    step = pl.program_id(0)

    @pl.when(step == 0)
    def _():
        total[...] = jnp.zeros_like(total)
        row = lax.broadcasted_iota(jnp.int32, (2 * PART, 2 * width), 0)
        col = lax.broadcasted_iota(jnp.int32, (2 * PART, 2 * width), 1)
        same = row // PART == col // width
        row, col = row % PART, col % width
        pick = (row < 24) & (row % 8 == col // PROBES) & (col < dirs)
        pick |= (row >= 24) & (row < 27) & (col >= dirs) & (col < dirs + 128)
        pick |= (row >= 27) & (row < 30) & (col >= dirs + 128)
        expand[...] = jnp.where(pick & same, 1.0, 0.0).astype(BF16)
        s = stiff_ref[...]
        stack[...] = jnp.zeros_like(stack)

        def put(value, at):
            where = pl.ds(at, ext_x, PART)
            stack[0, where, :] = value[:, :128]
            stack[1, where, :] = jnp.concatenate([value[:, 128:], jnp.zeros((ext_x, 256 - ext_y), F32)], axis=1)

        for g in range(shots):
            for part, value in enumerate(split3(field_ref[g, :ext_x, :] * s)):
                put(value, 8 * part + g)
        square = s * s
        for part, value in enumerate(split3(tau_step * square)):
            put(value, 24 + part)
        for part, value in enumerate(split3(1.0 / jnp.where(s > 0.0, square, 1.0))):
            put(value, 27 + part)
        words = jnp.concatenate(
            [field_ref[g, ext_x:ext_x + 8, :] for g in range(shots)], axis=0
        ).astype(BF16)
        row = lax.broadcasted_iota(jnp.int32, (8 * shots, dirs), 0)
        col = lax.broadcasted_iota(jnp.int32, (8 * shots, dirs), 1)

        def bits(offset, shift):
            probe = (col + shift) % PROBES
            hit = (row // 8 == col // PROBES) & (row % 8 - offset == probe // 8)
            value = lax.dot_general(words, jnp.where(hit, 1.0, 0.0).astype(BF16), TN, preferred_element_type=F32)
            lane = (lax.broadcasted_iota(jnp.int32, value.shape, 1) + shift) % 8
            bit = jnp.right_shift(value.astype(jnp.int32), lane) & 1
            return (2 * bit - 1).astype(F32)

        first[...] = bits(0, 0)[:ext_x]
        first_next[...] = 0.5 * bits(0, 1)[:ext_x]
        for ref, shift in ((second, 0), (second_next, 1)):
            value = bits(4, shift)
            for h in range(halves):
                spread[h] = value[:, 128 * h:128 * h + 128]
                for v in range(depth):
                    ref[h, v] = spread[h, pl.ds(v, 8, depth), :]

    def around(w):
        after = jnp.concatenate([w[1:], pltpu.roll(w[0], 7, 0)[None]], axis=0)
        before = jnp.concatenate([pltpu.roll(w[depth - 1], 1, 0)[None], w[:depth - 1]], axis=0)
        return after + before

    def stencil(src, at, dst):
        c = [coef[(at + k) & 7] for k in range(2)]
        keep = [1.0 - 4.0 * v for v in c]
        out = []
        for h in range(halves):
            w = [src[(at + k) & 3, h] for k in range(-1, 3)]
            for k in range(2):
                new = keep[k] * w[k + 1] + c[k] * ((w[k] + w[k + 2]) + around(w[k + 1]))
                if dst is None:
                    out.append(new)
                else:
                    dst[(at + k) & 3, h] = new
        return out

    def pair(p, _):
        i = step * ROWS + 2 * p
        rows = pl.ds(pl.multiple_of(i * PART, 2 * PART), 2 * PART)
        lhs = jnp.concatenate([stack[0, rows, :], stack[1, rows, :][:, :ext_y - 128]], axis=1).astype(BF16)
        wide = lax.dot_general(lhs, expand[...], TN, preferred_element_type=F32)
        for t in range(2 * width // 128):
            spread[t] = wide[:, 128 * t:128 * t + 128]
        gather = lambda t: jnp.stack([spread[t, pl.ds(v, 8, depth), :] for v in range(depth)])
        for k in range(2):
            at = i + k
            base = k * (width // 128)
            coef[at & 7] = gather(base + halves)
            back[at & 7] = gather(base + halves + 1)
            first_row, next_row = first[pl.ds(at, 1), :], first_next[pl.ds(at, 1), :]
            for h in range(halves):
                lanes = slice(128 * h, 128 * h + 128)
                scaled = gather(base + h)
                field[at & 7, h] = scaled
                probe = first_row[:, lanes][None] * second[h] + next_row[:, lanes][None] * second_next[h]
                w0[at & 3, h] = scaled * probe
        stencil(w0, i - 1, w1)
        stencil(w1, i - 2, w2)
        stencil(w2, i - 3, w3)
        last = stencil(w3, i - 4, None)
        for h in range(halves):
            for k in range(2):
                at = i - 4 + k
                value = field[at & 7, h] * (back[at & 7] * last[2 * h + k])
                for v in range(depth):
                    fold[2 * h + k, pl.ds(v, 8, depth), :] = value[v]
                lanes = slice(128 * h, 128 * h + 128)
                high_ref[2 * p + k, :, lanes], low_ref[2 * p + k, :, lanes] = split2(fold[2 * h + k, :ny])
        return 0

    lax.fori_loop(0, ROWS // 2, pair, 0)

    @pl.when(step > 0)
    def _():
        high = high_ref[...].reshape(ROWS * ny, dirs)
        low = low_ref[...].reshape(ROWS * ny, dirs)
        total[:, :dirs] += lax.dot_general(high, high, TN, preferred_element_type=F32)
        total[:, dirs:] += lax.dot_general(high, low, TN, preferred_element_type=F32)

    @pl.when(step == pl.num_programs(0) - 1)
    def _():
        cross = total[:, dirs:]
        total[:, :dirs] = total[:, :dirs] + cross + cross.T
        index = index_ref[0]
        strip = lambda at: total[pl.ds(pl.multiple_of(at * PROBES, PROBES), PROBES), :dirs]
        own_ref[...] = strip(index)
        other_ref[...] = strip(index ^ 1)


def responses(index, fields, stiffness, nx, ny):
    shots = fields.shape[0]
    dirs = shots * PROBES
    halves = dirs // 128
    ext_x, ext_y = nx + 2 * HALO, ny + 2 * HALO
    depth = ext_y // 8
    width = dirs + 256
    whole = lambda shape: pl.BlockSpec(shape, lambda s: (0,) * len(shape))
    block = pl.BlockSpec((ROWS, ny, dirs), lambda s: (jnp.maximum(s - 1, 0), 0, 0))
    return pl.pallas_call(
        functools.partial(response_kernel, shots, nx, ny),
        grid=(ext_x // ROWS,),
        in_specs=[SMEM, whole(fields.shape), whole(stiffness.shape)],
        out_specs=[whole((PROBES, dirs)), whole((PROBES, dirs)), block, block],
        out_shape=[
            jax.ShapeDtypeStruct((PROBES, dirs), F32),
            jax.ShapeDtypeStruct((PROBES, dirs), F32),
            jax.ShapeDtypeStruct((nx, ny, dirs), BF16),
            jax.ShapeDtypeStruct((nx, ny, dirs), BF16),
        ],
        scratch_shapes=[
            pltpu.VMEM((2 * PART, 2 * width), BF16),
            pltpu.VMEM((2, ext_x * PART, 128), F32),
            pltpu.VMEM((2 * width // 128, ext_y, 128), F32),
            pltpu.VMEM((ext_x, dirs), F32),
            pltpu.VMEM((ext_x, dirs), F32),
            pltpu.VMEM((halves, depth, 8, 128), F32),
            pltpu.VMEM((halves, depth, 8, 128), F32),
            pltpu.VMEM((8, depth, 8, 128), F32),
            pltpu.VMEM((8, depth, 8, 128), F32),
            pltpu.VMEM((8, halves, depth, 8, 128), F32),
            *[pltpu.VMEM((4, halves, depth, 8, 128), F32) for _ in range(4)],
            pltpu.VMEM((2 * halves, ext_y, 128), F32),
            pltpu.VMEM((dirs, 2 * dirs), F32),
        ],
        compiler_params=pltpu.CompilerParams(
            dimension_semantics=("arbitrary",), vmem_limit_bytes=48 * 2**20
        ),
        name="responses",
    )(index, fields, stiffness)


PANEL = 64
PIVOT = 4


def cholesky(n, gram_ref, table):
    tiles = n // 128
    eye_row = lax.broadcasted_iota(jnp.int32, (8, 128), 0)
    eye_col = lax.broadcasted_iota(jnp.int32, (8, 128), 1)
    table[:, :n] = gram_ref[...]
    full = lambda x: jnp.broadcast_to(x, (8, 128))
    for panel in range(n // PANEL):
        start = panel * PANEL
        tile = start // 128
        live = [*range(tile, tiles), *range(tiles, tiles + tile + 1)]
        rows = {}
        for g in range(PANEL // 8):
            for t in live:
                at = start + 8 * g
                value = None
                if t < tiles or panel > 0:
                    value = table[at:at + 8, 128 * t:128 * t + 128] if (t < tiles or (t - tiles) * 128 < start) else None
                if t >= tiles:
                    unit = (eye_row + at == eye_col + 128 * (t - tiles)).astype(F32)
                    value = unit if value is None else value + unit
                rows[g, t] = value
        for micro in range(PANEL // PIVOT):
            k = micro * PIVOT
            gp, r = k // 8, k % 8
            lane = (start + k) % 128
            pivot_rows = [{t: full(rows[gp, t][r + j:r + j + 1, :]) for t in live} for j in range(PIVOT)]
            a = {
                (i, j): full(pivot_rows[i][tile][:, lane + j:lane + j + 1])
                for i in range(PIVOT) for j in range(i + 1)
            }
            low, inv = {}, []
            for j in range(PIVOT):
                d = a[j, j]
                for m in range(j):
                    d = d - low[j, m] * low[j, m]
                inv.append(lax.rsqrt(d))
                for i in range(j + 1, PIVOT):
                    v = a[i, j]
                    for m in range(j):
                        v = v - low[i, m] * low[j, m]
                    low[i, j] = v * inv[j]
            ready = []
            for j in range(PIVOT):
                out = {}
                for t in live:
                    v = pivot_rows[j][t]
                    for m in range(j):
                        v = v - low[j, m] * ready[m][t]
                    out[t] = v * inv[j]
                ready.append(out)
            for g in range(gp, PANEL // 8):
                if g == gp and r + PIVOT == 8:
                    pass
                else:
                    cols = []
                    for j in range(PIVOT):
                        v = full(rows[g, tile][:, lane + j:lane + j + 1])
                        for m in range(j):
                            v = v - cols[m] * low[j, m]
                        cols.append(v * inv[j])
                    if g == gp:
                        cols = [jnp.where(eye_row >= r + PIVOT, v, 0.0) for v in cols]
                    for t in live:
                        v = rows[g, t]
                        for j in range(PIVOT):
                            v = v - cols[j] * ready[j][t]
                        rows[g, t] = v
                if g == gp:
                    for t in live:
                        v = rows[g, t]
                        for j in range(PIVOT):
                            v = jnp.where(eye_row == r + j, ready[j][t], v)
                        rows[g, t] = v
        for g in range(PANEL // 8):
            for t in live:
                at = start + 8 * g
                value = rows[g, t]
                if t == tile:
                    value = jnp.where(eye_row + at <= eye_col + 128 * t, value, 0.0)
                table[at:at + 8, 128 * t:128 * t + 128] = value
            for t in range(tile):
                table[start + 8 * g:start + 8 * g + 8, 128 * t:128 * t + 128] = jnp.zeros((8, 128), F32)
            for t in range(tiles + tile + 1, 2 * tiles):
                table[start + 8 * g:start + 8 * g + 8, 128 * t:128 * t + 128] = jnp.zeros((8, 128), F32)
        below = start + PANEL
        if below < n:
            keep = below // 128
            for t in range(keep, tiles + tile + 1):
                if t == keep:
                    lo = 128 * keep
                    left = table[start:below, lo:n]
                    p3 = [v.astype(BF16) for v in split3(left)]
                    lhs = jnp.concatenate([p3[0], p3[0], p3[1], p3[0], p3[2], p3[1]], axis=0)
                lanes = slice(128 * t, 128 * t + 128)
                right = [v.astype(BF16) for v in split3(table[start:below, lanes])]
                rhs = jnp.concatenate([right[0], right[1], right[0], right[2], right[0], right[1]], axis=0)
                update = lax.dot_general(lhs, rhs, TN, preferred_element_type=F32)[below - lo:]
                if t < tiles or 128 * (t - tiles) < start:
                    table[below:, lanes] = table[below:, lanes] - update
                else:
                    table[below:, lanes] = -update

def finish_kernel(n, scale, index_ref, gram_ref, high_hbm, low_hbm, upper_ref, own_ref, other_ref,
                  table, high_ref, low_ref, sems):
    copies = [
        pltpu.make_async_copy(high_hbm, high_ref, sems.at[0]),
        pltpu.make_async_copy(low_hbm, low_ref, sems.at[1]),
    ]
    for copy in copies:
        copy.start()
    cholesky(n, gram_ref, table)
    index = index_ref[0]
    strip = lambda at: pl.ds(pl.multiple_of(at * PROBES, PROBES), PROBES)
    upper_ref[...] = table[strip(index), :n] * (1.0 / scale)
    rows = jnp.concatenate([table[strip(index), n:], table[strip(index ^ 1), n:]], axis=0) * scale
    high, low = split2(rows)
    both = jnp.concatenate([high, low], axis=0)
    for copy in copies:
        copy.wait()
    count, ny = high_ref.shape[:2]
    for i in range(0, count, 2):
        main = lax.dot_general(both, high_ref[i:i + 2].reshape(2 * ny, n), NT, preferred_element_type=F32)
        rest = lax.dot_general(high, low_ref[i:i + 2].reshape(2 * ny, n), NT, preferred_element_type=F32)
        value = main[:2 * PROBES] + (main[2 * PROBES:] + rest)
        for k in range(2):
            own_ref[:, i + k, :] = value[:PROBES, ny * k:ny * k + ny]
            other_ref[:, i + k, :] = value[PROBES:, ny * k:ny * k + ny]


def finish(index, gram, high, low, scale):
    n = gram.shape[0]
    nx, ny = high.shape[:2]
    return pl.pallas_call(
        functools.partial(finish_kernel, n, scale),
        in_specs=[SMEM, VMEM, HBM, HBM],
        out_specs=[VMEM] * 3,
        out_shape=[
            jax.ShapeDtypeStruct((PROBES, n), F32),
            jax.ShapeDtypeStruct((PROBES, nx, ny), F32),
            jax.ShapeDtypeStruct((PROBES, nx, ny), F32),
        ],
        scratch_shapes=[
            pltpu.VMEM((n, 2 * n), F32),
            pltpu.VMEM(high.shape, BF16),
            pltpu.VMEM(low.shape, BF16),
            pltpu.SemaphoreType.DMA((2,)),
        ],
        compiler_params=pltpu.CompilerParams(vmem_limit_bytes=48 * 2**20),
        name="finish",
    )(index, gram, high, low)


def shards(signs_x, signs_y, heights, velocity, background):
    shots = lax.axis_size("dir")
    nx, ny = background.shape[1:]
    ext_x, ext_y = nx + 2 * HALO, ny + 2 * HALO
    half = nx // 2
    index = lax.axis_index("dir")
    which = index.reshape(1)
    stiffness, first, last = small(
        pack_x_kernel, [(nx, ny), (16, ny), (16, ny)], [VMEM] * 4, "pack_x"
    )(signs_x, heights, velocity, background)
    above, below = exchange(first, last, "sx")
    field, stiffness, octets, first, last = small(
        pack_y_kernel, [(ext_x, ny), (ext_x, ny), (8, ny), (ext_x + 8, ny), (ext_x + 8, ny)], [VMEM] * 6, "pack_y"
    )(signs_y, background, stiffness, first, above, below)
    left, right = exchange(first, last, "sy")
    send, stiffness = small(
        pack_dir_kernel, [(shots, half + 2 * HALO + 8, ext_y), (half + 2 * HALO, ext_y)], [SMEM] + [VMEM] * 6, "pack_dir"
    )(which, field, stiffness, octets, first, left, right)
    fields = lax.all_to_all(send, "dir", 0, 0)
    own, other, high, low = responses(which, fields, stiffness, half, ny)
    swap = [(i, i ^ 1) for i in range(shots)]
    dirs = shots * PROBES
    strip = own + lax.ppermute(other, "dir", swap)
    terms = lax.all_to_all(strip.reshape(PROBES, dirs // 128, 128), ("sx", "sy"), 0, 0)
    row = jnp.sum(terms, axis=0, keepdims=True)
    gram = lax.all_to_all(jnp.broadcast_to(row, (dirs, *row.shape[1:])), ("dir", "sx", "sy"), 0, 0)
    gram = gram.reshape(dirs, dirs)
    scale = math.sqrt(nx * ny * lax.axis_size("sx") * lax.axis_size("sy"))
    factor, own, other = finish(which, gram, high, low, scale)
    other = lax.ppermute(other, "dir", swap)
    upper = index & 1 == 1
    basis = jnp.concatenate([jnp.where(upper, other, own), jnp.where(upper, own, other)], axis=1)
    return basis, factor


def solution(mesh):
    in_specs = (P("dir", "sx"), P("dir", "sy"), P("sx", "sy"), P("sx", "sy"), P("dir", "sx", "sy"))
    out_specs = (P("dir", "sx", "sy"), P("dir", None))
    return jax.shard_map(shards, mesh=mesh, in_specs=in_specs, out_specs=out_specs, check_vma=False)
```

time: 146 us -> 122 us (0.84)
  blocking collectives: 42.2 us -> 59.5 us
  Pallas kernels: 52.9 us -> 37.5 us
  waiting for transfers between devices: 19 us -> 4.74 us
  local copies, waits for them, and re-layouts: 9.71 us -> 5.01 us
  starting transfers between devices: 17.6 us -> 12.9 us
  other arithmetic: 2.95 us -> 1.22 us
    pallas_call x1, Pallas kernels: 35.9 us -> 19.5 us  [responses(): pl.pallas_call(functools.partial(response_kernel, shots, nx, ny), grid=(e...]
    all_to_all x0 -> x1, blocking collectives: none -> 15.9 us  [shards(): fields = lax.all_to_all(send, 'dir', 0, 0)]
    all_to_all x1 -> x0, waiting for transfers between devices: 9.73 us -> none  [shards(): lax.all_to_all(jnp.broadcast_to(own[None], (shots, *own.shape)), 'dir', 0...]
    all_to_all x1 -> x0, starting transfers between devices: 7.41 us -> none  [shards(): lax.all_to_all(jnp.broadcast_to(own[None], (shots, *own.shape)), 'dir', 0...]
    ppermute x4 -> x6, waiting for transfers between devices: 9.26 us -> 4.74 us  [the longest x2 2.34 us: exchange(): before = lax.ppermute(last, axis, [(i, i + 1) for i in range(count - 1)])]
    unnamed x9 -> x15, local copies, waits for them, and re-layouts: 8.06 us -> 4.91 us
    ppermute x4 -> x6, starting transfers between devices: 10.2 us -> 12.9 us  [the longest x2 8.99 us: exchange(): before = lax.ppermute(last, axis, [(i, i + 1) for i in range(count - 1)])]
    convert_element_type x3 -> x0, other arithmetic: 2.23 us -> none  [the longest x2 1.46 us: as_bytes(): return (jnp.right_shift(words[None, :], shifts[:, None]) & 255).astype(F32)]
  transfers between devices with their start and end apart: 5 -> 6, of which waited for: 4 -> 4; matrix products, arithmetic and copies ran while one was open for 1% -> 0% of each run, Pallas kernels for 0% -> 0%
where the time goes in v2:
time: 122 us
  blocking collectives  59.5 us (49%)
  Pallas kernels  37.5 us (31%)
  starting transfers between devices  12.9 us (11%)
  local copies, waits for them, and re-layouts  5.01 us (4%)
  waiting for transfers between devices  4.74 us (4%)
  other arithmetic  1.22 us (1%)
    all_to_all x1, blocking collectives, shards(): lax.all_to_all(jnp.broadcast_to(row, (dirs, *row.shape[1:])), ('dir', 'sx...  22.3 us
    all_to_all x1, blocking collectives, shards(): lax.all_to_all(strip.reshape(PROBES, dirs // 128, 128), ('sx', 'sy'), 0, 0)  21.3 us
    pallas_call x1, Pallas kernels, responses(): pl.pallas_call(functools.partial(response_kernel, shots, nx, ny), grid=(e...  19.5 us
    all_to_all x1, blocking collectives, shards(): fields = lax.all_to_all(send, 'dir', 0, 0)  15.9 us
    pallas_call x1, Pallas kernels, finish(): pl.pallas_call(functools.partial(finish_kernel, n, scale), in_specs=[SMEM...  13.3 us
    ppermute x2, starting transfers between devices, exchange(): before = lax.ppermute(last, axis, [(i, i + 1) for i in range(count - 1)])  8.99 us
    unnamed x15, local copies, waits for them, and re-layouts  4.91 us
    ppermute x2, starting transfers between devices, exchange(): after = lax.ppermute(first, axis, [(i + 1, i) for i in range(count - 1)])  2.56 us
  transfers between devices with their start and end apart: 6, of which 4 were waited for; matrix products, arithmetic and copies ran while one was open for 0% of the time, Pallas kernels for 0%

profile of v2, /device:TPU:1, one launch (start us, length us, event | category | flops | bytes accessed | tf_op | source)
XLA Modules:
  0.0 121.6 jit_solution(9893827805134312949)
XLA Ops:
  0.6 1.4 %pack_x.1 = (f32[64,128]{1,0:T(8,128)}, f32[16,128]{1,0:T(8,128)}, f32[16,128]{1,0:T(8,128)}) custom-call(s32[1,64]{1,0:T(1,128)} %signs_ref.2, s32[64,128]{1,0:T(8,128)} %heights_ref.1, f32[64,128]{1,0:T(8,128)} %velocity_ref.1, f32[1,64,128]{2,1,0:T(8,128)} %field_ref.3), custom_call_target="tpu_custom_call" | custom-call | tf_op jit(solution)/shard_map/pack_x/pallas_call | solution.py:465
  2.1 1.3 %collective-permute-start.1 = (f32[16,128]{1,0:T(8,128)}, f32[16,128]{1,0:T(8,128)S(1)}, u32[]{:S(2)}, u32[]{:S(2)}) collective-permute-start(f32[16,128]{1,0:T(8,128)} %get-tuple-element.20.own_ref), channel_id=1, source_target_pairs={{8,0},{16,8},{24,16},{9,1},{17,9},{25,17},{10,2},{18,10},{26,18},{... | collective-permute-start | bytes 24584 | tf_op jit(solution)/shard_map/ppermute | solution.py:121
  3.4 4.7 %collective-permute-start = (f32[16,128]{1,0:T(8,128)}, f32[16,128]{1,0:T(8,128)S(1)}, u32[]{:S(2)}, u32[]{:S(2)}) collective-permute-start(f32[16,128]{1,0:T(8,128)} %get-tuple-element.21), channel_id=1, source_target_pairs={{0,8},{8,16},{16,24},{1,9},{9,17},{17,25},{2,10},{10,18},{18,26},{... | collective-permute-start | bytes 24584 | tf_op jit(solution)/shard_map/ppermute | solution.py:120
  8.0 1.0 collective-permute-done.above_ref
  9.0 0.6 copy-done.6
  9.6 1.5 %pack_y.1 = (f32[72,128]{1,0:T(8,128)}, f32[72,128]{1,0:T(8,128)}, f32[8,128]{1,0:T(8,128)}, f32[80,128]{1,0:T(8,128)}, f32[80,128]{1,0:T(8,128)}) custom-call(s32[1,128]{1,0:T(1,128)} %signs_ref.3, f32[1,64,128]{2,1,0:T(8,128)} %field_ref.3, f32[64,128]{1,0:T(8,128)} %get-tuple-element.19.stiff_ref, f32[16,128]{1,0:T(8,128)} %get-tuple-element.20.own_ref, ...), custom_call_target="tpu_custom_call" | custom-call | tf_op jit(solution)/shard_map/pack_y/pallas_call | solution.py:469
  11.1 1.3 %collective-permute-start.3 = (f32[80,128]{1,0:T(8,128)}, f32[80,128]{1,0:T(8,128)S(1)}, u32[]{:S(2)}, u32[]{:S(2)}) collective-permute-start(f32[80,128]{1,0:T(8,128)} %get-tuple-element.25.own_ref), channel_id=1, source_target_pairs={{1,0},{2,1},{3,2},{4,3},{5,4},{6,5},{7,6},{9,8},{10,9},{11,10},{12... | collective-permute-start | bytes 122888 | tf_op jit(solution)/shard_map/ppermute | solution.py:121
  12.4 4.3 %collective-permute-start.2 = (f32[80,128]{1,0:T(8,128)}, f32[80,128]{1,0:T(8,128)S(1)}, u32[]{:S(2)}, u32[]{:S(2)}) collective-permute-start(f32[80,128]{1,0:T(8,128)} %get-tuple-element.26), channel_id=1, source_target_pairs={{0,1},{1,2},{2,3},{3,4},{4,5},{5,6},{6,7},{8,9},{9,10},{10,11},{11... | collective-permute-start | bytes 122888 | tf_op jit(solution)/shard_map/ppermute | solution.py:120
  16.8 1.4 %collective-permute-done.2.left_ref = f32[80,128]{1,0:T(8,128)S(1)} collective-permute-done((f32[80,128]{1,0:T(8,128)}, f32[80,128]{1,0:T(8,128)S(1)}, u32[]{:S(2)}, u32[]{:S(2)}) %collective-permute-start.2) | collective-permute-done | bytes 40992 | tf_op jit(solution)/shard_map/ppermute | solution.py:120
  18.2 0.6 copy-done.4
  18.8 1.7 %pack_dir.1 = (f32[8,48,136]{2,1,0:T(8,128)}, f32[40,136]{1,0:T(8,128)}) custom-call(s32[1]{0:T(128)} %bitcast.index_ref, f32[72,128]{1,0:T(8,128)} %get-tuple-element.22.field_ref, f32[72,128]{1,0:T(8,128)} %get-tuple-element.23.stiff_ref, f32[8,128]{1,0:T(8,128)} %get-tuple-element.24.octets_ref, f32[80,128]{1,0:T(8,128)} %get-tuple-element.25.own_ref, ...), custom_call_target="tpu_custom_call" | custom-call | tf_op jit(solution)/shard_map/pack_dir/pallas_call | solution.py:473
  20.5 15.9 %all_to_all.15.field_ref = f32[8,48,136]{2,1,0:T(8,128)S(1)} all-to-all(f32[8,48,136]{2,1,0:T(8,128)} %get-tuple-element.27), channel_id=1, replica_groups=mesh['dir'=8,'sx'=4,'sy'=8] {'dir'}, dimensions={0} | all-to-all | bytes 417792 | tf_op jit(solution)/shard_map/all_to_all | solution.py:476
  36.4 0.8 copy-done.2
  37.2 19.5 %responses.1 = (f32[32,256]{1,0:T(8,128)S(1)}, f32[32,256]{1,0:T(8,128)S(1)}, bf16[32,128,256]{2,1,0:T(8,128)(2,1)S(1)}, bf16[32,128,256]{2,1,0:T(8,128)(2,1)S(1)}) custom-call(s32[1]{0:T(128)} %bitcast.index_ref, f32[8,48,136]{2,1,0:T(8,128)S(1)} %all_to_all.15.field_ref, f32[40,136]{1,0:T(8,128)S(1)} %copy-done.2), custom_call_target="tpu_custom_call" | custom-call | tf_op jit(solution)/shard_map/responses/pallas_call | solution.py:269
  56.7 1.3 %copy-done = bf16[32,128,256]{2,1,0:T(8,128)(2,1)} copy-done((bf16[32,128,256]{2,1,0:T(8,128)(2,1)}, bf16[32,128,256]{2,1,0:T(8,128)(2,1)S(1)}, u32[]{:S(2)}) %copy-start) | copy-done | bytes 2097176
  58.0 0.9 collective-permute-start.4
  58.9 0.9 collective-permute-done.4
  59.8 21.3 %all_to_all.16 = f32[32,2,128]{2,1,0:T(2,128)S(1)} all-to-all(f32[32,2,128]{2,1,0:T(2,128)S(1)} %reshape.15), channel_id=1, replica_groups=mesh['dir'=8,'sx'=4,'sy'=8] {'sx','sy'}, dimensions={0} | all-to-all | bytes 65536 | tf_op jit(solution)/shard_map/all_to_all | solution.py:481
  81.2 22.3 %all_to_all.17 = f32[256,2,128]{2,1,0:T(2,128)S(1)} all-to-all(f32[256,2,128]{2,1,0:T(2,128)S(1)} %broadcast_in_dim.2), channel_id=1, replica_groups=mesh['dir'=8,'sx'=4,'sy'=8] {'dir','sx','sy'}, dimensions={0} | all-to-all | bytes 524288 | tf_op jit(solution)/shard_map/all_to_all | solution.py:483
  103.5 1.6 %copy-done.1 = bf16[32,128,256]{2,1,0:T(8,128)(2,1)S(1)} copy-done((bf16[32,128,256]{2,1,0:T(8,128)(2,1)S(1)}, bf16[32,128,256]{2,1,0:T(8,128)(2,1)}, u32[]{:S(2)}) %copy-start.1) | copy-done | bytes 2097176
  105.1 13.3 %finish.1 = (f32[32,256]{1,0:T(8,128)}, f32[32,32,128]{2,1,0:T(8,128)S(1)}, f32[32,32,128]{2,1,0:T(8,128)S(1)}) custom-call(s32[1]{0:T(128)} %bitcast.index_ref, f32[256,256]{1,0:T(8,128)S(1)} %bitcast.5, bf16[32,128,256]{2,1,0:T(8,128)(2,1)S(1)} %get-tuple-element.31.high_hbm, bf16[32,128,256]{2,1,0:T(8,128)(2,1)S(1)} %copy-done.1), custom_call_target="tpu_custom_call" | custom-call | tf_op jit(solution)/shard_map/finish/pallas_call | solution.py:438
  118.4 0.5 collective-permute-start.5
  118.9 1.5 %collective-permute-done.5 = f32[32,32,128]{2,1,0:T(8,128)S(1)} collective-permute-done((f32[32,32,128]{2,1,0:T(8,128)S(1)}, f32[32,32,128]{2,1,0:T(8,128)S(1)}, u32[]{:S(2)}, u32[]{:S(2)}) %collective-permute-start.5) | collective-permute-done | bytes 524320 | tf_op jit(solution)/shard_map/ppermute | solution.py:487
  120.6 1.1 pad_maximum_fusion
  (17 shorter events, 0.3 us)
Async XLA Ops:
  2.1 6.0 %collective-permute-start.1 = (f32[16,128]{1,0:T(8,128)}, f32[16,128]{1,0:T(8,128)S(1)}, u32[]{:S(2)}, u32[]{:S(2)}) collective-permute-start(f32[16,128]{1,0:T(8,128)} %get-tuple-element.20.own_ref), channel_id=1, source_target_pairs={{8,0},{16,8},{24,16},{9,1},{17,9},{25,17},{10,2},{18,10},{26,18},{... | collective-permute-start | bytes 24584 | tf_op jit(solution)/shard_map/ppermute | solution.py:121
  3.4 5.7 %collective-permute-start = (f32[16,128]{1,0:T(8,128)}, f32[16,128]{1,0:T(8,128)S(1)}, u32[]{:S(2)}, u32[]{:S(2)}) collective-permute-start(f32[16,128]{1,0:T(8,128)} %get-tuple-element.21), channel_id=1, source_target_pairs={{0,8},{8,16},{16,24},{1,9},{9,17},{17,25},{2,10},{10,18},{18,26},{... | collective-permute-start | bytes 24584 | tf_op jit(solution)/shard_map/ppermute | solution.py:120
  8.0 1.0 copy-start.5
  9.0 0.6 copy-start.6
  11.1 5.6 %collective-permute-start.3 = (f32[80,128]{1,0:T(8,128)}, f32[80,128]{1,0:T(8,128)S(1)}, u32[]{:S(2)}, u32[]{:S(2)}) collective-permute-start(f32[80,128]{1,0:T(8,128)} %get-tuple-element.25.own_ref), channel_id=1, source_target_pairs={{1,0},{2,1},{3,2},{4,3},{5,4},{6,5},{7,6},{9,8},{10,9},{11,10},{12... | collective-permute-start | bytes 122888 | tf_op jit(solution)/shard_map/ppermute | solution.py:121
  12.4 5.7 %collective-permute-start.2 = (f32[80,128]{1,0:T(8,128)}, f32[80,128]{1,0:T(8,128)S(1)}, u32[]{:S(2)}, u32[]{:S(2)}) collective-permute-start(f32[80,128]{1,0:T(8,128)} %get-tuple-element.26), channel_id=1, source_target_pairs={{0,1},{1,2},{2,3},{3,4},{4,5},{5,6},{6,7},{8,9},{9,10},{10,11},{11... | collective-permute-start | bytes 122888 | tf_op jit(solution)/shard_map/ppermute | solution.py:120
  16.8 1.4 %copy-start.3 = (f32[80,128]{1,0:T(8,128)}, f32[80,128]{1,0:T(8,128)S(1)}, u32[]{:S(2)}) copy-start(f32[80,128]{1,0:T(8,128)S(1)} %collective-permute-done.3.right_ref) | copy-start | bytes 122884
  18.2 0.6 copy-start.4
  36.4 0.8 copy-start.2
  56.7 1.3 %copy-start = (bf16[32,128,256]{2,1,0:T(8,128)(2,1)}, bf16[32,128,256]{2,1,0:T(8,128)(2,1)S(1)}, u32[]{:S(2)}) copy-start(bf16[32,128,256]{2,1,0:T(8,128)(2,1)S(1)} %get-tuple-element.32.low_hbm) | copy-start | bytes 6291460
  58.0 1.7 %collective-permute-start.4 = (f32[32,256]{1,0:T(8,128)S(1)}, f32[32,256]{1,0:T(8,128)S(1)}, u32[]{:S(2)}, u32[]{:S(2)}) collective-permute-start(f32[32,256]{1,0:T(8,128)S(1)} %get-tuple-element.30), channel_id=1, source_target_pairs={{0,32},{32,0},{64,96},{96,64},{128,160},{160,128},{192,224},{224,1... | collective-permute-start | bytes 98312 | tf_op jit(solution)/shard_map/ppermute | solution.py:480
  103.5 1.6 %copy-start.1 = (bf16[32,128,256]{2,1,0:T(8,128)(2,1)S(1)}, bf16[32,128,256]{2,1,0:T(8,128)(2,1)}, u32[]{:S(2)}) copy-start(bf16[32,128,256]{2,1,0:T(8,128)(2,1)} %copy-done) | copy-start | bytes 6291460
  118.4 2.0 %collective-permute-start.5 = (f32[32,32,128]{2,1,0:T(8,128)S(1)}, f32[32,32,128]{2,1,0:T(8,128)S(1)}, u32[]{:S(2)}, u32[]{:S(2)}) collective-permute-start(f32[32,32,128]{2,1,0:T(8,128)S(1)} %get-tuple-element.33), channel_id=1, source_target_pairs={{0,32},{32,0},{64,96},{96,64},{128,160},{160,128},{192,224},{224,1... | collective-permute-start | bytes 1572872 | tf_op jit(solution)/shard_map/ppermute | solution.py:487

commit v3 on v2

--- a/solution.py
+++ b/solution.py
@@ -20,7 +20,6 @@
 NT = (((1,), (1,)), ((), ()))
 VMEM = pl.BlockSpec(memory_space=pltpu.VMEM)
 SMEM = pl.BlockSpec(memory_space=pltpu.SMEM)
-HBM = pl.BlockSpec(memory_space=pltpu.HBM)
 
 
 def split2(x):
@@ -111,6 +110,7 @@
         in_specs=specs,
         out_specs=[VMEM] * len(shapes),
         out_shape=[jax.ShapeDtypeStruct(shape, F32) for shape in shapes],
+        compiler_params=pltpu.CompilerParams(vmem_limit_bytes=4 * 2**20),
         name=name,
     )
 
@@ -125,15 +125,26 @@
 PART = 32
 
 
-def response_kernel(shots, nx, ny, index_ref, field_ref, stiff_ref, own_ref, other_ref, high_ref, low_ref,
+def response_kernel(shots, nx, ny, index_ref, field_ref, stiff_ref, own_ref, other_ref, parts_ref,
                     expand, stack, spread, first, first_next, second, second_next,
-                    coef, back, field, w0, w1, w2, w3, fold, total):
+                    w0, w1, w2, w3, fold, total):
     dirs = shots * PROBES
     halves = dirs // 128
     ext_x, ext_y = nx + 2 * HALO, ny + 2 * HALO
-    depth = ext_y // 8
+    depth = ny // 8
     width = dirs + 256
     step = pl.program_id(0)
+    sub = lax.broadcasted_iota(jnp.int32, (8, 128), 0)
+
+    def at_cell(slot, t, v):
+        return spread[slot, t, pl.ds(v, 8, depth), :] if v < depth else spread[slot, t, ny:ext_y, :]
+
+    def widen(i, slot):
+        rows = pl.ds(pl.multiple_of(i * PART, 2 * PART), 2 * PART)
+        lhs = jnp.concatenate([stack[0, rows, :], stack[1, rows, :][:, :ext_y - 128]], axis=1).astype(BF16)
+        wide = lax.dot_general(lhs, expand[...], TN, preferred_element_type=F32)
+        for t in range(2 * width // 128):
+            spread[slot, t] = wide[:, 128 * t:128 * t + 128]
 
     @pl.when(step == 0)
     def _():
@@ -181,71 +192,93 @@
         for ref, shift in ((second, 0), (second_next, 1)):
             value = bits(4, shift)
             for h in range(halves):
-                spread[h] = value[:, 128 * h:128 * h + 128]
-                for v in range(depth):
-                    ref[h, v] = spread[h, pl.ds(v, 8, depth), :]
-
-    def around(w):
-        after = jnp.concatenate([w[1:], pltpu.roll(w[0], 7, 0)[None]], axis=0)
-        before = jnp.concatenate([pltpu.roll(w[depth - 1], 1, 0)[None], w[:depth - 1]], axis=0)
-        return after + before
-
-    def stencil(src, at, dst):
-        c = [coef[(at + k) & 7] for k in range(2)]
-        keep = [1.0 - 4.0 * v for v in c]
-        out = []
+                spread[0, h] = value[:, 128 * h:128 * h + 128]
+                for v in range(depth + 1):
+                    ref[h, v] = at_cell(0, h, v)
+        widen(0, 0)
+
+    pairs = ROWS // 2
+    count = width // 128
+
+    def place(row):
+        return (row >> 1) & (pairs - 1), (row & 1) * count
+
+    def stencil(src, at, emit):
+        centre, upper, lower, edge = {}, {}, {}, {}
         for h in range(halves):
-            w = [src[(at + k) & 3, h] for k in range(-1, 3)]
             for k in range(2):
-                new = keep[k] * w[k + 1] + c[k] * ((w[k] + w[k + 2]) + around(w[k + 1]))
-                if dst is None:
-                    out.append(new)
-                else:
-                    dst[(at + k) & 3, h] = new
-        return out
-
-    def pair(p, _):
-        i = step * ROWS + 2 * p
-        rows = pl.ds(pl.multiple_of(i * PART, 2 * PART), 2 * PART)
-        lhs = jnp.concatenate([stack[0, rows, :], stack[1, rows, :][:, :ext_y - 128]], axis=1).astype(BF16)
-        wide = lax.dot_general(lhs, expand[...], TN, preferred_element_type=F32)
-        for t in range(2 * width // 128):
-            spread[t] = wide[:, 128 * t:128 * t + 128]
-        gather = lambda t: jnp.stack([spread[t, pl.ds(v, 8, depth), :] for v in range(depth)])
-        for k in range(2):
-            at = i + k
-            base = k * (width // 128)
-            coef[at & 7] = gather(base + halves)
-            back[at & 7] = gather(base + halves + 1)
-            first_row, next_row = first[pl.ds(at, 1), :], first_next[pl.ds(at, 1), :]
+                ref = src.at[(at + k) & 3, h]
+                head, tail, halo = ref[0], ref[depth - 1], ref[depth]
+                head_up, halo_up = pltpu.roll(head, 7, 0), pltpu.roll(halo, 7, 0)
+                tail_down, halo_down = pltpu.roll(tail, 1, 0), pltpu.roll(halo, 1, 0)
+                edge[h, k] = jnp.where(sub == 7, halo_up, head_up)
+                after_halo = jnp.where(sub == 7, head_up, halo_up)
+                before_head = jnp.where(sub == 0, halo_down, tail_down)
+                before_halo = jnp.where(sub == 0, tail_down, halo_down)
+                lower[h, k], centre[h, k] = before_head, head
+                upper[h, k] = after_halo + before_halo
+        for v in range(depth + 1):
+            c = [at_cell(*[place(at + k)[0], place(at + k)[1] + halves], v) for k in range(2)]
+            for h in range(halves):
+                above = src[(at - 1) & 3, h, v]
+                below = src[(at + 2) & 3, h, v]
+                if v == depth:
+                    for k in range(2):
+                        centre[h, k] = src[(at + k) & 3, h, v]
+                mid = [centre[h, k] for k in range(2)]
+                for k in range(2):
+                    if v < depth:
+                        after = src[(at + k) & 3, h, v + 1] if v < depth - 1 else edge[h, k]
+                        side = after + lower[h, k]
+                        lower[h, k], centre[h, k] = mid[k], after
+                    else:
+                        side = upper[h, k]
+                    beside = (above + mid[1]) if k == 0 else (mid[0] + below)
+                    emit(k, h, v, mid[k] + c[k] * ((beside + side) - 4.0 * mid[k]))
+
+    def level(src, at, dst):
+        def emit(k, h, v, value):
+            dst[(at + k) & 3, h, v] = value
+        stencil(src, at, emit)
+
+    for p in range(pairs):
+        i = 2 * p
+        first_row = [first[pl.ds(step * ROWS + i + k, 1), :] for k in range(2)]
+        next_row = [first_next[pl.ds(step * ROWS + i + k, 1), :] for k in range(2)]
+        for v in range(depth + 1):
             for h in range(halves):
                 lanes = slice(128 * h, 128 * h + 128)
-                scaled = gather(base + h)
-                field[at & 7, h] = scaled
-                probe = first_row[:, lanes][None] * second[h] + next_row[:, lanes][None] * second_next[h]
-                w0[at & 3, h] = scaled * probe
-        stencil(w0, i - 1, w1)
-        stencil(w1, i - 2, w2)
-        stencil(w2, i - 3, w3)
-        last = stencil(w3, i - 4, None)
+                one, two = second[h, v], second_next[h, v]
+                for k in range(2):
+                    probe = first_row[k][:, lanes] * one + next_row[k][:, lanes] * two
+                    slot, tile = place(i + k)
+                    w0[(i + k) & 3, h, v] = at_cell(slot, tile + h, v) * probe
+        widen(jnp.minimum(step * ROWS + i + 2, ext_x - 2), (p + 1) % pairs)
+        level(w0, i - 1, w1)
+        level(w1, i - 2, w2)
+        level(w2, i - 3, w3)
+
+        def emit(k, h, v, value):
+            if v < depth:
+                slot, tile = place(i - 4 + k)
+                scale = at_cell(slot, tile + h, v) * at_cell(slot, tile + halves + 1, v)
+                fold[2 * h + k, 8 * v:8 * v + 8, :] = scale * value
+
+        stencil(w3, i - 4, emit)
         for h in range(halves):
             for k in range(2):
-                at = i - 4 + k
-                value = field[at & 7, h] * (back[at & 7] * last[2 * h + k])
-                for v in range(depth):
-                    fold[2 * h + k, pl.ds(v, 8, depth), :] = value[v]
-                lanes = slice(128 * h, 128 * h + 128)
-                high_ref[2 * p + k, :, lanes], low_ref[2 * p + k, :, lanes] = split2(fold[2 * h + k, :ny])
-        return 0
-
-    lax.fori_loop(0, ROWS // 2, pair, 0)
+                for q in range(0, depth, 2):
+                    value = jnp.concatenate(
+                        [fold[2 * h + k, pl.ds(8 * (r % depth) + r // depth, 8, 8), :] for r in (8 * q, 8 * q + 8)], axis=0
+                    )
+                    for part, piece in enumerate(split2(value)):
+                        at_lane = part * dirs + 128 * h
+                        parts_ref[i + k, 8 * q:8 * q + 16, at_lane:at_lane + 128] = piece
 
     @pl.when(step > 0)
     def _():
-        high = high_ref[...].reshape(ROWS * ny, dirs)
-        low = low_ref[...].reshape(ROWS * ny, dirs)
-        total[:, :dirs] += lax.dot_general(high, high, TN, preferred_element_type=F32)
-        total[:, dirs:] += lax.dot_general(high, low, TN, preferred_element_type=F32)
+        parts = parts_ref[...].reshape(ROWS * ny, 2 * dirs)
+        total[...] += lax.dot_general(parts[:, :dirs], parts, TN, preferred_element_type=F32)
 
     @pl.when(step == pl.num_programs(0) - 1)
     def _():
@@ -262,45 +295,41 @@
     dirs = shots * PROBES
     halves = dirs // 128
     ext_x, ext_y = nx + 2 * HALO, ny + 2 * HALO
-    depth = ext_y // 8
+    blocks = ext_y // 8
     width = dirs + 256
     whole = lambda shape: pl.BlockSpec(shape, lambda s: (0,) * len(shape))
-    block = pl.BlockSpec((ROWS, ny, dirs), lambda s: (jnp.maximum(s - 1, 0), 0, 0))
+    block = pl.BlockSpec((ROWS, ny, 2 * dirs), lambda s: (jnp.maximum(s - 1, 0), 0, 0))
     return pl.pallas_call(
         functools.partial(response_kernel, shots, nx, ny),
         grid=(ext_x // ROWS,),
         in_specs=[SMEM, whole(fields.shape), whole(stiffness.shape)],
-        out_specs=[whole((PROBES, dirs)), whole((PROBES, dirs)), block, block],
+        out_specs=[whole((PROBES, dirs)), whole((PROBES, dirs)), block],
         out_shape=[
             jax.ShapeDtypeStruct((PROBES, dirs), F32),
             jax.ShapeDtypeStruct((PROBES, dirs), F32),
-            jax.ShapeDtypeStruct((nx, ny, dirs), BF16),
-            jax.ShapeDtypeStruct((nx, ny, dirs), BF16),
+            jax.ShapeDtypeStruct((nx, ny, 2 * dirs), BF16),
         ],
         scratch_shapes=[
             pltpu.VMEM((2 * PART, 2 * width), BF16),
             pltpu.VMEM((2, ext_x * PART, 128), F32),
-            pltpu.VMEM((2 * width // 128, ext_y, 128), F32),
+            pltpu.VMEM((ROWS // 2, 2 * width // 128, ext_y, 128), F32),
             pltpu.VMEM((ext_x, dirs), F32),
             pltpu.VMEM((ext_x, dirs), F32),
-            pltpu.VMEM((halves, depth, 8, 128), F32),
-            pltpu.VMEM((halves, depth, 8, 128), F32),
-            pltpu.VMEM((8, depth, 8, 128), F32),
-            pltpu.VMEM((8, depth, 8, 128), F32),
-            pltpu.VMEM((8, halves, depth, 8, 128), F32),
-            *[pltpu.VMEM((4, halves, depth, 8, 128), F32) for _ in range(4)],
-            pltpu.VMEM((2 * halves, ext_y, 128), F32),
+            pltpu.VMEM((halves, blocks, 8, 128), F32),
+            pltpu.VMEM((halves, blocks, 8, 128), F32),
+            *[pltpu.VMEM((4, halves, blocks, 8, 128), F32) for _ in range(4)],
+            pltpu.VMEM((2 * halves, ny, 128), F32),
             pltpu.VMEM((dirs, 2 * dirs), F32),
         ],
         compiler_params=pltpu.CompilerParams(
-            dimension_semantics=("arbitrary",), vmem_limit_bytes=48 * 2**20
+            dimension_semantics=("arbitrary",), vmem_limit_bytes=61 * 2**20
         ),
         name="responses",
     )(index, fields, stiffness)
 
 
 PANEL = 64
-PIVOT = 4
+PIVOT = 8
 
 
 def cholesky(n, gram_ref, table):
@@ -405,14 +434,9 @@
                 else:
                     table[below:, lanes] = -update
 
-def finish_kernel(n, scale, index_ref, gram_ref, high_hbm, low_hbm, upper_ref, own_ref, other_ref,
-                  table, high_ref, low_ref, sems):
-    copies = [
-        pltpu.make_async_copy(high_hbm, high_ref, sems.at[0]),
-        pltpu.make_async_copy(low_hbm, low_ref, sems.at[1]),
-    ]
-    for copy in copies:
-        copy.start()
+def finish_kernel(n, scale, index_ref, gram_ref, parts_any, upper_ref, own_ref, other_ref, table, parts_ref, sem):
+    copy = pltpu.make_async_copy(parts_any, parts_ref, sem)
+    copy.start()
     cholesky(n, gram_ref, table)
     index = index_ref[0]
     strip = lambda at: pl.ds(pl.multiple_of(at * PROBES, PROBES), PROBES)
@@ -420,24 +444,24 @@
     rows = jnp.concatenate([table[strip(index), n:], table[strip(index ^ 1), n:]], axis=0) * scale
     high, low = split2(rows)
     both = jnp.concatenate([high, low], axis=0)
-    for copy in copies:
-        copy.wait()
-    count, ny = high_ref.shape[:2]
+    copy.wait()
+    count, ny = parts_ref.shape[:2]
     for i in range(0, count, 2):
-        main = lax.dot_general(both, high_ref[i:i + 2].reshape(2 * ny, n), NT, preferred_element_type=F32)
-        rest = lax.dot_general(high, low_ref[i:i + 2].reshape(2 * ny, n), NT, preferred_element_type=F32)
+        parts = parts_ref[i:i + 2].reshape(2 * ny, 2 * n)
+        main = lax.dot_general(both, parts[:, :n], NT, preferred_element_type=F32)
+        rest = lax.dot_general(high, parts[:, n:], NT, preferred_element_type=F32)
         value = main[:2 * PROBES] + (main[2 * PROBES:] + rest)
         for k in range(2):
             own_ref[:, i + k, :] = value[:PROBES, ny * k:ny * k + ny]
             other_ref[:, i + k, :] = value[PROBES:, ny * k:ny * k + ny]
 
 
-def finish(index, gram, high, low, scale):
+def finish(index, gram, parts, scale):
     n = gram.shape[0]
-    nx, ny = high.shape[:2]
+    nx, ny = parts.shape[:2]
     return pl.pallas_call(
         functools.partial(finish_kernel, n, scale),
-        in_specs=[SMEM, VMEM, HBM, HBM],
+        in_specs=[SMEM, VMEM, pl.BlockSpec(memory_space=pl.ANY)],
         out_specs=[VMEM] * 3,
         out_shape=[
             jax.ShapeDtypeStruct((PROBES, n), F32),
@@ -446,13 +470,12 @@
         ],
         scratch_shapes=[
             pltpu.VMEM((n, 2 * n), F32),
-            pltpu.VMEM(high.shape, BF16),
-            pltpu.VMEM(low.shape, BF16),
-            pltpu.SemaphoreType.DMA((2,)),
+            pltpu.VMEM(parts.shape, BF16),
+            pltpu.SemaphoreType.DMA,
         ],
-        compiler_params=pltpu.CompilerParams(vmem_limit_bytes=48 * 2**20),
+        compiler_params=pltpu.CompilerParams(vmem_limit_bytes=61 * 2**20),
         name="finish",
-    )(index, gram, high, low)
+    )(index, gram, parts)
 
 
 def shards(signs_x, signs_y, heights, velocity, background):
@@ -474,7 +497,7 @@
         pack_dir_kernel, [(shots, half + 2 * HALO + 8, ext_y), (half + 2 * HALO, ext_y)], [SMEM] + [VMEM] * 6, "pack_dir"
     )(which, field, stiffness, octets, first, left, right)
     fields = lax.all_to_all(send, "dir", 0, 0)
-    own, other, high, low = responses(which, fields, stiffness, half, ny)
+    own, other, parts = responses(which, fields, stiffness, half, ny)
     swap = [(i, i ^ 1) for i in range(shots)]
     dirs = shots * PROBES
     strip = own + lax.ppermute(other, "dir", swap)
@@ -483,7 +506,7 @@
     gram = lax.all_to_all(jnp.broadcast_to(row, (dirs, *row.shape[1:])), ("dir", "sx", "sy"), 0, 0)
     gram = gram.reshape(dirs, dirs)
     scale = math.sqrt(nx * ny * lax.axis_size("sx") * lax.axis_size("sy"))
-    factor, own, other = finish(which, gram, high, low, scale)
+    factor, own, other = finish(which, gram, parts, scale)
     other = lax.ppermute(other, "dir", swap)
     upper = index & 1 == 1
     basis = jnp.concatenate([jnp.where(upper, other, own), jnp.where(upper, own, other)], axis=1)

time: 122 us -> 122 us (level)
  Pallas kernels: 37.5 us -> 35.1 us
  other arithmetic: 1.22 us -> 3 us
    pallas_call x1, Pallas kernels: 1.71 us -> 0.09 us  [shards(): small(pack_dir_kernel, [(shots, half + 2 * HALO + 8, ext_y), (half + 2 *...]
    pallas_call x1, Pallas kernels: 19.5 us -> 21.1 us  [responses(): pl.pallas_call(functools.partial(response_kernel, shots, nx, ny), grid=(e...]
    pallas_call x1, Pallas kernels: 1.54 us -> 0.1 us  [shards(): small(pack_y_kernel, [(ext_x, ny), (ext_x, ny), (8, ny), (ext_x + 8, ny),...]
    pallas_call x1, Pallas kernels: 1.44 us -> 0.02 us  [shards(): small(pack_x_kernel, [(nx, ny), (16, ny), (16, ny)], [VMEM] * 4, 'pack_x')]
where the time goes in v3:
time: 122 us; the launch traced here: 121 us
  blocking collectives  59.5 us (49%)
  Pallas kernels  35.1 us (29%)
  starting transfers between devices  12.9 us (11%)
  local copies, waits for them, and re-layouts  5.16 us (4%)
  waiting for transfers between devices  4.65 us (4%)
  other arithmetic  3 us (2%)
    all_to_all x1, blocking collectives, shards(): lax.all_to_all(jnp.broadcast_to(row, (dirs, *row.shape[1:])), ('dir', 'sx...  22.3 us
    all_to_all x1, blocking collectives, shards(): lax.all_to_all(strip.reshape(PROBES, dirs // 128, 128), ('sx', 'sy'), 0, 0)  21.6 us
    pallas_call x1, Pallas kernels, responses(): pl.pallas_call(functools.partial(response_kernel, shots, nx, ny), grid=(e...  21.1 us
    all_to_all x1, blocking collectives, shards(): fields = lax.all_to_all(send, 'dir', 0, 0)  15.6 us
    pallas_call x1, Pallas kernels, finish(): pl.pallas_call(functools.partial(finish_kernel, n, scale), in_specs=[SMEM...  13.8 us
    ppermute x2, starting transfers between devices, exchange(): before = lax.ppermute(last, axis, [(i, i + 1) for i in range(count - 1)])  8.99 us
    unnamed x15, local copies, waits for them, and re-layouts  5.07 us
    ppermute x2, starting transfers between devices, exchange(): after = lax.ppermute(first, axis, [(i + 1, i) for i in range(count - 1)])  2.58 us
  transfers between devices with their start and end apart: 6, of which 4 were waited for; matrix products, arithmetic and copies ran while one was open for 0% of the time, Pallas kernels for 0%

profile of v3, /device:TPU:1, one launch (start us, length us, event | category | flops | bytes accessed | tf_op | source)
XLA Modules:
  0.0 121.1 jit_solution(16412384977603491660)
XLA Ops:
  0.6 0.7 copy-done
  1.4 0.8 copy-done.3
  2.2 0.8 copy-done.4
  2.9 0.7 copy-done.5
  3.6 1.3 %collective-permute-start.1 = (f32[16,128]{1,0:T(8,128)S(1)}, f32[16,128]{1,0:T(8,128)S(1)}, u32[]{:S(2)}, u32[]{:S(2)}) collective-permute-start(f32[16,128]{1,0:T(8,128)S(1)} %get-tuple-element.19.own_ref), channel_id=1, source_target_pairs={{8,0},{16,8},{24,16},{9,1},{17,9},{25,17},{10,2},{18,10},{26,18},{... | collective-permute-start | bytes 24584 | tf_op jit(solution)/shard_map/ppermute | solution.py:121
  4.9 4.7 %collective-permute-start = (f32[16,128]{1,0:T(8,128)S(1)}, f32[16,128]{1,0:T(8,128)S(1)}, u32[]{:S(2)}, u32[]{:S(2)}) collective-permute-start(f32[16,128]{1,0:T(8,128)S(1)} %get-tuple-element.20), channel_id=1, source_target_pairs={{0,8},{8,16},{16,24},{1,9},{9,17},{17,25},{2,10},{10,18},{18,26},{... | collective-permute-start | bytes 24584 | tf_op jit(solution)/shard_map/ppermute | solution.py:120
  9.6 0.8 collective-permute-done.above_ref
  10.3 0.8 copy-done.1
  11.1 0.7 copy-done.6
  11.9 1.3 %collective-permute-start.3 = (f32[80,128]{1,0:T(8,128)S(1)}, f32[80,128]{1,0:T(8,128)S(1)}, u32[]{:S(2)}, u32[]{:S(2)}) collective-permute-start(f32[80,128]{1,0:T(8,128)S(1)} %get-tuple-element.24.own_ref), channel_id=1, source_target_pairs={{1,0},{2,1},{3,2},{4,3},{5,4},{6,5},{7,6},{9,8},{10,9},{11,10},{12... | collective-permute-start | bytes 122888 | tf_op jit(solution)/shard_map/ppermute | solution.py:121
  13.2 4.3 %collective-permute-start.2 = (f32[80,128]{1,0:T(8,128)S(1)}, f32[80,128]{1,0:T(8,128)S(1)}, u32[]{:S(2)}, u32[]{:S(2)}) collective-permute-start(f32[80,128]{1,0:T(8,128)S(1)} %get-tuple-element.25), channel_id=1, source_target_pairs={{0,1},{1,2},{2,3},{3,4},{4,5},{5,6},{6,7},{8,9},{9,10},{10,11},{11... | collective-permute-start | bytes 122888 | tf_op jit(solution)/shard_map/ppermute | solution.py:120
  17.5 1.1 collective-permute-done.2.left_ref
  18.7 15.6 %all_to_all.15.field_ref = f32[8,48,136]{2,1,0:T(8,128)} all-to-all(f32[8,48,136]{2,1,0:T(8,128)S(1)} %get-tuple-element.26), channel_id=1, replica_groups=mesh['dir'=8,'sx'=4,'sy'=8] {'dir'}, dimensions={0} | all-to-all | bytes 417792 | tf_op jit(solution)/shard_map/all_to_all | solution.py:499
  34.3 21.1 %responses.1 = (f32[32,256]{1,0:T(8,128)}, f32[32,256]{1,0:T(8,128)}, bf16[32,128,512]{2,1,0:T(8,128)(2,1)}) custom-call(s32[1]{0:T(128)} %bitcast.index_ref, f32[8,48,136]{2,1,0:T(8,128)} %all_to_all.15.field_ref, f32[40,136]{1,0:T(8,128)} %copy-done.2), custom_call_target="tpu_custom_call" | custom-call | tf_op jit(solution)/shard_map/responses/pallas_call | solution.py:302
  55.4 0.9 collective-permute-start.4
  56.3 1.1 collective-permute-done.4
  57.3 0.8 add.3
  58.1 21.6 %all_to_all.16 = f32[32,2,128]{2,1,0:T(2,128)S(1)} all-to-all(f32[32,2,128]{2,1,0:T(2,128)S(1)} %reshape.15), channel_id=1, replica_groups=mesh['dir'=8,'sx'=4,'sy'=8] {'sx','sy'}, dimensions={0} | all-to-all | bytes 65536 | tf_op jit(solution)/shard_map/all_to_all | solution.py:504
  79.8 22.3 %all_to_all.17 = f32[256,2,128]{2,1,0:T(2,128)S(1)} all-to-all(f32[256,2,128]{2,1,0:T(2,128)S(1)} %broadcast_in_dim.2), channel_id=1, replica_groups=mesh['dir'=8,'sx'=4,'sy'=8] {'dir','sx','sy'}, dimensions={0} | all-to-all | bytes 524288 | tf_op jit(solution)/shard_map/all_to_all | solution.py:506
  102.1 0.7 copy.9
  102.8 13.8 %finish.1 = (f32[32,256]{1,0:T(8,128)}, f32[32,32,128]{2,1,0:T(8,128)}, f32[32,32,128]{2,1,0:T(8,128)}) custom-call(s32[1]{0:T(128)} %bitcast.index_ref, f32[256,256]{1,0:T(8,128)} %bitcast.5, bf16[32,128,512]{2,1,0:T(8,128)(2,1)} %get-tuple-element.30.parts_any), custom_call_target="tpu_custom_call" | custom-call | tf_op jit(solution)/shard_map/finish/pallas_call | solution.py:462
  117.1 1.7 %collective-permute-done.5 = f32[32,32,128]{2,1,0:T(8,128)S(1)} collective-permute-done((f32[32,32,128]{2,1,0:T(8,128)}, f32[32,32,128]{2,1,0:T(8,128)S(1)}, u32[]{:S(2)}, u32[]{:S(2)}) %collective-permute-start.5) | collective-permute-done | bytes 524320 | tf_op jit(solution)/shard_map/ppermute | solution.py:510
  118.9 1.1 broadcast_select_fusion.1
  120.0 1.1 pad_maximum_fusion
  (17 shorter events, 0.9 us)
Async XLA Ops:
  0.6 0.8 copy-start
  1.4 0.8 copy-start.3
  2.1 0.8 copy-start.4
  2.9 0.7 copy-start.5
  3.6 6.0 %collective-permute-start.1 = (f32[16,128]{1,0:T(8,128)S(1)}, f32[16,128]{1,0:T(8,128)S(1)}, u32[]{:S(2)}, u32[]{:S(2)}) collective-permute-start(f32[16,128]{1,0:T(8,128)S(1)} %get-tuple-element.19.own_ref), channel_id=1, source_target_pairs={{8,0},{16,8},{24,16},{9,1},{17,9},{25,17},{10,2},{18,10},{26,18},{... | collective-permute-start | bytes 24584 | tf_op jit(solution)/shard_map/ppermute | solution.py:121
  4.9 5.4 %collective-permute-start = (f32[16,128]{1,0:T(8,128)S(1)}, f32[16,128]{1,0:T(8,128)S(1)}, u32[]{:S(2)}, u32[]{:S(2)}) collective-permute-start(f32[16,128]{1,0:T(8,128)S(1)} %get-tuple-element.20), channel_id=1, source_target_pairs={{0,8},{8,16},{16,24},{1,9},{9,17},{17,25},{2,10},{10,18},{18,26},{... | collective-permute-start | bytes 24584 | tf_op jit(solution)/shard_map/ppermute | solution.py:120
  10.3 0.8 copy-start.1
  11.1 0.7 copy-start.6
  11.9 5.6 %collective-permute-start.3 = (f32[80,128]{1,0:T(8,128)S(1)}, f32[80,128]{1,0:T(8,128)S(1)}, u32[]{:S(2)}, u32[]{:S(2)}) collective-permute-start(f32[80,128]{1,0:T(8,128)S(1)} %get-tuple-element.24.own_ref), channel_id=1, source_target_pairs={{1,0},{2,1},{3,2},{4,3},{5,4},{6,5},{7,6},{9,8},{10,9},{11,10},{12... | collective-permute-start | bytes 122888 | tf_op jit(solution)/shard_map/ppermute | solution.py:121
  13.2 5.4 %collective-permute-start.2 = (f32[80,128]{1,0:T(8,128)S(1)}, f32[80,128]{1,0:T(8,128)S(1)}, u32[]{:S(2)}, u32[]{:S(2)}) collective-permute-start(f32[80,128]{1,0:T(8,128)S(1)} %get-tuple-element.25), channel_id=1, source_target_pairs={{0,1},{1,2},{2,3},{3,4},{4,5},{5,6},{6,7},{8,9},{9,10},{10,11},{11... | collective-permute-start | bytes 122888 | tf_op jit(solution)/shard_map/ppermute | solution.py:120
  18.7 15.7 %copy-start.2 = (f32[40,136]{1,0:T(8,128)}, f32[40,136]{1,0:T(8,128)S(1)}, u32[]{:S(2)}) copy-start(f32[40,136]{1,0:T(8,128)S(1)} %get-tuple-element.27.stiff_ref) | copy-start | bytes 65284
  55.4 2.0 %collective-permute-start.4 = (f32[32,256]{1,0:T(8,128)}, f32[32,256]{1,0:T(8,128)S(1)}, u32[]{:S(2)}, u32[]{:S(2)}) collective-permute-start(f32[32,256]{1,0:T(8,128)} %get-tuple-element.29), channel_id=1, source_target_pairs={{0,32},{32,0},{64,96},{96,64},{128,160},{160,128},{192,224},{224,1... | collective-permute-start | bytes 98312 | tf_op jit(solution)/shard_map/ppermute | solution.py:503
  116.6 2.2 %collective-permute-start.5 = (f32[32,32,128]{2,1,0:T(8,128)}, f32[32,32,128]{2,1,0:T(8,128)S(1)}, u32[]{:S(2)}, u32[]{:S(2)}) collective-permute-start(f32[32,32,128]{2,1,0:T(8,128)} %get-tuple-element.31), channel_id=1, source_target_pairs={{0,32},{32,0},{64,96},{96,64},{128,160},{160,128},{192,224},{224,1... | collective-permute-start | bytes 1572872 | tf_op jit(solution)/shard_map/ppermute | solution.py:510

commit v4 on v3

--- a/solution.py
+++ b/solution.py
@@ -104,13 +104,13 @@
     stiff_out[:, ny:] = spare[:, :2 * HALO]
 
 
-def small(kernel, shapes, specs, name):
+def small(kernel, shapes, specs, name, limit=4):
     return pl.pallas_call(
         kernel,
         in_specs=specs,
         out_specs=[VMEM] * len(shapes),
         out_shape=[jax.ShapeDtypeStruct(shape, F32) for shape in shapes],
-        compiler_params=pltpu.CompilerParams(vmem_limit_bytes=4 * 2**20),
+        compiler_params=pltpu.CompilerParams(vmem_limit_bytes=limit * 2**20),
         name=name,
     )
 
@@ -137,14 +137,19 @@
     sub = lax.broadcasted_iota(jnp.int32, (8, 128), 0)
 
     def at_cell(slot, t, v):
-        return spread[slot, t, pl.ds(v, 8, depth), :] if v < depth else spread[slot, t, ny:ext_y, :]
+        return spread[slot, t, pl.ds(v, 8, depth + 1), :] if v < depth else spread[slot, t, ny + 8:ext_y + 8, :]
+
+    def lay(slot, t, value):
+        for y in range(0, ext_y, 8):
+            at = y + y // depth if y < ny else y + 8
+            spread[slot, t, at:at + 8, :] = value[y:y + 8]
 
     def widen(i, slot):
         rows = pl.ds(pl.multiple_of(i * PART, 2 * PART), 2 * PART)
         lhs = jnp.concatenate([stack[0, rows, :], stack[1, rows, :][:, :ext_y - 128]], axis=1).astype(BF16)
         wide = lax.dot_general(lhs, expand[...], TN, preferred_element_type=F32)
         for t in range(2 * width // 128):
-            spread[slot, t] = wide[:, 128 * t:128 * t + 128]
+            lay(slot, t, wide[:, 128 * t:128 * t + 128])
 
     @pl.when(step == 0)
     def _():
@@ -192,7 +197,7 @@
         for ref, shift in ((second, 0), (second_next, 1)):
             value = bits(4, shift)
             for h in range(halves):
-                spread[0, h] = value[:, 128 * h:128 * h + 128]
+                lay(0, h, value[:, 128 * h:128 * h + 128])
                 for v in range(depth + 1):
                     ref[h, v] = at_cell(0, h, v)
         widen(0, 0)
@@ -262,14 +267,14 @@
             if v < depth:
                 slot, tile = place(i - 4 + k)
                 scale = at_cell(slot, tile + h, v) * at_cell(slot, tile + halves + 1, v)
-                fold[2 * h + k, 8 * v:8 * v + 8, :] = scale * value
+                fold[2 * h + k, 9 * v:9 * v + 8, :] = scale * value
 
         stencil(w3, i - 4, emit)
         for h in range(halves):
             for k in range(2):
                 for q in range(0, depth, 2):
                     value = jnp.concatenate(
-                        [fold[2 * h + k, pl.ds(8 * (r % depth) + r // depth, 8, 8), :] for r in (8 * q, 8 * q + 8)], axis=0
+                        [fold[2 * h + k, pl.ds(9 * (r % depth) + r // depth, 8, 9), :] for r in (8 * q, 8 * q + 8)], axis=0
                     )
                     for part, piece in enumerate(split2(value)):
                         at_lane = part * dirs + 128 * h
@@ -312,13 +317,13 @@
         scratch_shapes=[
             pltpu.VMEM((2 * PART, 2 * width), BF16),
             pltpu.VMEM((2, ext_x * PART, 128), F32),
-            pltpu.VMEM((ROWS // 2, 2 * width // 128, ext_y, 128), F32),
+            pltpu.VMEM((ROWS // 2, 2 * width // 128, ext_y + 8, 128), F32),
             pltpu.VMEM((ext_x, dirs), F32),
             pltpu.VMEM((ext_x, dirs), F32),
             pltpu.VMEM((halves, blocks, 8, 128), F32),
             pltpu.VMEM((halves, blocks, 8, 128), F32),
             *[pltpu.VMEM((4, halves, blocks, 8, 128), F32) for _ in range(4)],
-            pltpu.VMEM((2 * halves, ny, 128), F32),
+            pltpu.VMEM((2 * halves, ny + 2 * 8, 128), F32),
             pltpu.VMEM((dirs, 2 * dirs), F32),
         ],
         compiler_params=pltpu.CompilerParams(
@@ -473,7 +478,7 @@
             pltpu.VMEM(parts.shape, BF16),
             pltpu.SemaphoreType.DMA,
         ],
-        compiler_params=pltpu.CompilerParams(vmem_limit_bytes=61 * 2**20),
+        compiler_params=pltpu.CompilerParams(vmem_limit_bytes=16 * 2**20),
         name="finish",
     )(index, gram, parts)
 
@@ -486,7 +491,7 @@
     index = lax.axis_index("dir")
     which = index.reshape(1)
     stiffness, first, last = small(
-        pack_x_kernel, [(nx, ny), (16, ny), (16, ny)], [VMEM] * 4, "pack_x"
+        pack_x_kernel, [(nx, ny), (16, ny), (16, ny)], [VMEM] * 4, "pack_x", 60
     )(signs_x, heights, velocity, background)
     above, below = exchange(first, last, "sx")
     field, stiffness, octets, first, last = small(

time: 122 us -> 113 us (0.926)
  Pallas kernels: 35.1 us -> 27 us
    pallas_call x1, Pallas kernels: 21.1 us -> 15.2 us  [responses(): pl.pallas_call(functools.partial(response_kernel, shots, nx, ny), grid=(e...]
    pallas_call x1, Pallas kernels: 13.8 us -> 10.1 us  [finish(): pl.pallas_call(functools.partial(finish_kernel, n, scale), in_specs=[SMEM...]
    pallas_call x1, Pallas kernels: 0.02 us -> 1.44 us  [shards(): small(pack_x_kernel, [(nx, ny), (16, ny), (16, ny)], [VMEM] * 4, 'pack_x'...]
    unnamed x15 -> x13, local copies, waits for them, and re-layouts: 5.07 us -> 5.07 us
where the time goes in v4:
time: 113 us; the launch traced here: 112 us
  blocking collectives  59.5 us (53%)
  Pallas kernels  27 us (24%)
  starting transfers between devices  12.9 us (11%)
  local copies, waits for them, and re-layouts  5.16 us (5%)
  waiting for transfers between devices  4.65 us (4%)
  other arithmetic  1.98 us (2%)
    all_to_all x1, blocking collectives, shards(): lax.all_to_all(jnp.broadcast_to(row, (dirs, *row.shape[1:])), ('dir', 'sx...  22.3 us
    all_to_all x1, blocking collectives, shards(): lax.all_to_all(strip.reshape(PROBES, dirs // 128, 128), ('sx', 'sy'), 0, 0)  21.6 us
    all_to_all x1, blocking collectives, shards(): fields = lax.all_to_all(send, 'dir', 0, 0)  15.6 us
    pallas_call x1, Pallas kernels, responses(): pl.pallas_call(functools.partial(response_kernel, shots, nx, ny), grid=(e...  15.2 us
    pallas_call x1, Pallas kernels, finish(): pl.pallas_call(functools.partial(finish_kernel, n, scale), in_specs=[SMEM...  10.1 us
    ppermute x2, starting transfers between devices, exchange(): before = lax.ppermute(last, axis, [(i, i + 1) for i in range(count - 1)])  8.99 us
    unnamed x13, local copies, waits for them, and re-layouts  5.07 us
    ppermute x2, starting transfers between devices, exchange(): after = lax.ppermute(first, axis, [(i + 1, i) for i in range(count - 1)])  2.57 us
  transfers between devices with their start and end apart: 6, of which 4 were waited for; matrix products, arithmetic and copies ran while one was open for 0% of the time, Pallas kernels for 0%

profile of v4, /device:TPU:1, one launch (start us, length us, event | category | flops | bytes accessed | tf_op | source)
XLA Modules:
  0.0 111.9 jit_solution(7203974652066081527)
XLA Ops:
  0.6 1.4 %pack_x.1 = (f32[64,128]{1,0:T(8,128)}, f32[16,128]{1,0:T(8,128)}, f32[16,128]{1,0:T(8,128)}) custom-call(s32[1,64]{1,0:T(1,128)} %signs_ref.2, s32[64,128]{1,0:T(8,128)} %heights_ref.1, f32[64,128]{1,0:T(8,128)} %velocity_ref.1, f32[1,64,128]{2,1,0:T(8,128)} %field_ref.3), custom_call_target="tpu_custom_call" | custom-call | tf_op jit(solution)/shard_map/pack_x/pallas_call | solution.py:493
  2.1 1.3 %collective-permute-start.1 = (f32[16,128]{1,0:T(8,128)}, f32[16,128]{1,0:T(8,128)S(1)}, u32[]{:S(2)}, u32[]{:S(2)}) collective-permute-start(f32[16,128]{1,0:T(8,128)} %get-tuple-element.19.own_ref), channel_id=1, source_target_pairs={{8,0},{16,8},{24,16},{9,1},{17,9},{25,17},{10,2},{18,10},{26,18},{... | collective-permute-start | bytes 24584 | tf_op jit(solution)/shard_map/ppermute | solution.py:121
  3.4 4.7 %collective-permute-start = (f32[16,128]{1,0:T(8,128)}, f32[16,128]{1,0:T(8,128)S(1)}, u32[]{:S(2)}, u32[]{:S(2)}) collective-permute-start(f32[16,128]{1,0:T(8,128)} %get-tuple-element.20), channel_id=1, source_target_pairs={{0,8},{8,16},{16,24},{1,9},{9,17},{17,25},{2,10},{10,18},{18,26},{... | collective-permute-start | bytes 24584 | tf_op jit(solution)/shard_map/ppermute | solution.py:120
  8.0 1.0 collective-permute-done.above_ref
  9.0 0.8 copy-done.1
  9.8 0.8 copy-done.3
  10.5 0.7 copy-done.4
  11.2 0.7 copy-done.5
  12.0 1.3 %collective-permute-start.3 = (f32[80,128]{1,0:T(8,128)S(1)}, f32[80,128]{1,0:T(8,128)S(1)}, u32[]{:S(2)}, u32[]{:S(2)}) collective-permute-start(f32[80,128]{1,0:T(8,128)S(1)} %get-tuple-element.24.own_ref), channel_id=1, source_target_pairs={{1,0},{2,1},{3,2},{4,3},{5,4},{6,5},{7,6},{9,8},{10,9},{11,10},{12... | collective-permute-start | bytes 122888 | tf_op jit(solution)/shard_map/ppermute | solution.py:121
  13.3 4.3 %collective-permute-start.2 = (f32[80,128]{1,0:T(8,128)S(1)}, f32[80,128]{1,0:T(8,128)S(1)}, u32[]{:S(2)}, u32[]{:S(2)}) collective-permute-start(f32[80,128]{1,0:T(8,128)S(1)} %get-tuple-element.25), channel_id=1, source_target_pairs={{0,1},{1,2},{2,3},{3,4},{4,5},{5,6},{6,7},{8,9},{9,10},{10,11},{11... | collective-permute-start | bytes 122888 | tf_op jit(solution)/shard_map/ppermute | solution.py:120
  17.6 1.1 collective-permute-done.2.left_ref
  18.8 15.6 %all_to_all.15.field_ref = f32[8,48,136]{2,1,0:T(8,128)} all-to-all(f32[8,48,136]{2,1,0:T(8,128)S(1)} %get-tuple-element.26), channel_id=1, replica_groups=mesh['dir'=8,'sx'=4,'sy'=8] {'dir'}, dimensions={0} | all-to-all | bytes 417792 | tf_op jit(solution)/shard_map/all_to_all | solution.py:504
  34.5 15.2 %responses.1 = (f32[32,256]{1,0:T(8,128)}, f32[32,256]{1,0:T(8,128)}, bf16[32,128,512]{2,1,0:T(8,128)(2,1)}) custom-call(s32[1]{0:T(128)} %bitcast.index_ref, f32[8,48,136]{2,1,0:T(8,128)} %all_to_all.15.field_ref, f32[40,136]{1,0:T(8,128)} %copy-done.2), custom_call_target="tpu_custom_call" | custom-call | tf_op jit(solution)/shard_map/responses/pallas_call | solution.py:307
  49.7 0.9 collective-permute-start.4
  50.6 1.1 collective-permute-done.4
  51.6 0.8 add.3
  52.4 21.6 %all_to_all.16 = f32[32,2,128]{2,1,0:T(2,128)S(1)} all-to-all(f32[32,2,128]{2,1,0:T(2,128)S(1)} %reshape.15), channel_id=1, replica_groups=mesh['dir'=8,'sx'=4,'sy'=8] {'sx','sy'}, dimensions={0} | all-to-all | bytes 65536 | tf_op jit(solution)/shard_map/all_to_all | solution.py:509
  74.1 22.3 %all_to_all.17 = f32[256,2,128]{2,1,0:T(2,128)S(1)} all-to-all(f32[256,2,128]{2,1,0:T(2,128)S(1)} %broadcast_in_dim.2), channel_id=1, replica_groups=mesh['dir'=8,'sx'=4,'sy'=8] {'dir','sx','sy'}, dimensions={0} | all-to-all | bytes 524288 | tf_op jit(solution)/shard_map/all_to_all | solution.py:511
  96.4 2.2 %copy-done = bf16[32,128,512]{2,1,0:T(8,128)(2,1)S(1)} copy-done((bf16[32,128,512]{2,1,0:T(8,128)(2,1)S(1)}, bf16[32,128,512]{2,1,0:T(8,128)(2,1)}, u32[]{:S(2)}) %copy-start) | copy-done | bytes 4194328
  98.6 10.1 %finish.1 = (f32[32,256]{1,0:T(8,128)}, f32[32,32,128]{2,1,0:T(8,128)S(1)}, f32[32,32,128]{2,1,0:T(8,128)S(1)}) custom-call(s32[1]{0:T(128)} %bitcast.index_ref, f32[256,256]{1,0:T(8,128)S(1)} %bitcast.5, bf16[32,128,512]{2,1,0:T(8,128)(2,1)S(1)} %copy-done), custom_call_target="tpu_custom_call" | custom-call | tf_op jit(solution)/shard_map/finish/pallas_call | solution.py:467
  108.7 0.5 collective-permute-start.5
  109.2 1.5 %collective-permute-done.5 = f32[32,32,128]{2,1,0:T(8,128)S(1)} collective-permute-done((f32[32,32,128]{2,1,0:T(8,128)S(1)}, f32[32,32,128]{2,1,0:T(8,128)S(1)}, u32[]{:S(2)}, u32[]{:S(2)}) %collective-permute-start.5) | collective-permute-done | bytes 524320 | tf_op jit(solution)/shard_map/ppermute | solution.py:515
  110.8 0.1 broadcast_select_fusion.1
  110.9 1.1 pad_maximum_fusion
  (15 shorter events, 0.4 us)
Async XLA Ops:
  2.1 6.0 %collective-permute-start.1 = (f32[16,128]{1,0:T(8,128)}, f32[16,128]{1,0:T(8,128)S(1)}, u32[]{:S(2)}, u32[]{:S(2)}) collective-permute-start(f32[16,128]{1,0:T(8,128)} %get-tuple-element.19.own_ref), channel_id=1, source_target_pairs={{8,0},{16,8},{24,16},{9,1},{17,9},{25,17},{10,2},{18,10},{26,18},{... | collective-permute-start | bytes 24584 | tf_op jit(solution)/shard_map/ppermute | solution.py:121
  3.4 5.7 %collective-permute-start = (f32[16,128]{1,0:T(8,128)}, f32[16,128]{1,0:T(8,128)S(1)}, u32[]{:S(2)}, u32[]{:S(2)}) collective-permute-start(f32[16,128]{1,0:T(8,128)} %get-tuple-element.20), channel_id=1, source_target_pairs={{0,8},{8,16},{16,24},{1,9},{9,17},{17,25},{2,10},{10,18},{18,26},{... | collective-permute-start | bytes 24584 | tf_op jit(solution)/shard_map/ppermute | solution.py:120
  9.0 0.8 copy-start.1
  9.8 0.8 copy-start.3
  10.5 0.7 copy-start.4
  11.2 0.7 copy-start.5
  12.0 5.6 %collective-permute-start.3 = (f32[80,128]{1,0:T(8,128)S(1)}, f32[80,128]{1,0:T(8,128)S(1)}, u32[]{:S(2)}, u32[]{:S(2)}) collective-permute-start(f32[80,128]{1,0:T(8,128)S(1)} %get-tuple-element.24.own_ref), channel_id=1, source_target_pairs={{1,0},{2,1},{3,2},{4,3},{5,4},{6,5},{7,6},{9,8},{10,9},{11,10},{12... | collective-permute-start | bytes 122888 | tf_op jit(solution)/shard_map/ppermute | solution.py:121
  13.3 5.4 %collective-permute-start.2 = (f32[80,128]{1,0:T(8,128)S(1)}, f32[80,128]{1,0:T(8,128)S(1)}, u32[]{:S(2)}, u32[]{:S(2)}) collective-permute-start(f32[80,128]{1,0:T(8,128)S(1)} %get-tuple-element.25), channel_id=1, source_target_pairs={{0,1},{1,2},{2,3},{3,4},{4,5},{5,6},{6,7},{8,9},{9,10},{10,11},{11... | collective-permute-start | bytes 122888 | tf_op jit(solution)/shard_map/ppermute | solution.py:120
  18.8 15.7 %copy-start.2 = (f32[40,136]{1,0:T(8,128)}, f32[40,136]{1,0:T(8,128)S(1)}, u32[]{:S(2)}) copy-start(f32[40,136]{1,0:T(8,128)S(1)} %get-tuple-element.27.stiff_ref) | copy-start | bytes 65284
  49.7 1.9 %collective-permute-start.4 = (f32[32,256]{1,0:T(8,128)}, f32[32,256]{1,0:T(8,128)S(1)}, u32[]{:S(2)}, u32[]{:S(2)}) collective-permute-start(f32[32,256]{1,0:T(8,128)} %get-tuple-element.29), channel_id=1, source_target_pairs={{0,32},{32,0},{64,96},{96,64},{128,160},{160,128},{192,224},{224,1... | collective-permute-start | bytes 98312 | tf_op jit(solution)/shard_map/ppermute | solution.py:508
  96.4 2.2 %copy-start = (bf16[32,128,512]{2,1,0:T(8,128)(2,1)S(1)}, bf16[32,128,512]{2,1,0:T(8,128)(2,1)}, u32[]{:S(2)}) copy-start(bf16[32,128,512]{2,1,0:T(8,128)(2,1)} %get-tuple-element.30.parts_any) | copy-start | bytes 12582916
  108.7 2.0 %collective-permute-start.5 = (f32[32,32,128]{2,1,0:T(8,128)S(1)}, f32[32,32,128]{2,1,0:T(8,128)S(1)}, u32[]{:S(2)}, u32[]{:S(2)}) collective-permute-start(f32[32,32,128]{2,1,0:T(8,128)S(1)} %get-tuple-element.31), channel_id=1, source_target_pairs={{0,32},{32,0},{64,96},{96,64},{128,160},{160,128},{192,224},{224,1... | collective-permute-start | bytes 1572872 | tf_op jit(solution)/shard_map/ppermute | solution.py:515

commit v5 on v4

--- a/solution.py
+++ b/solution.py
@@ -40,11 +40,15 @@
     return (jnp.right_shift(jnp.broadcast_to(words, shape), shift) & 255).astype(F32)
 
 
-def pack_x_kernel(signs_ref, heights_ref, velocity_ref, field_ref, stiff_ref, first_ref, last_ref):
+def pack_x_kernel(signs_ref, other_signs_ref, heights_ref, velocity_ref, field_ref, body_ref, first_ref, last_ref):
     nx, ny = velocity_ref.shape
     stiff = velocity_ref[...] * jnp.sqrt(1.0 + heights_ref[...].astype(F32) / LEVELS)
-    stiff_ref[...] = stiff
     octets = sign_bytes(signs_ref[...])
+    body_ref[0:nx, :] = field_ref[0]
+    body_ref[nx:2 * nx, :] = stiff
+    body_ref[2 * nx:2 * nx + 8, :] = jnp.zeros((8, ny), F32)
+    body_ref[2 * nx:2 * nx + 8, :nx] = octets
+    body_ref[2 * nx + 8:, :] = sign_bytes(other_signs_ref[...])
     for ref, start in ((first_ref, 0), (last_ref, nx - HALO)):
         ref[0:HALO, :] = field_ref[0, start:start + HALO, :]
         ref[HALO:2 * HALO, :] = stiff[start:start + HALO]
@@ -52,22 +56,22 @@
         ref[8:16, :nx] = octets
 
 
-def pack_y_kernel(signs_ref, field_ref, stiff_ref, own_ref, above_ref, below_ref,
+def pack_y_kernel(body_ref, above_ref, below_ref,
                   field_out, stiff_out, octets_out, first_ref, last_ref):
-    nx, ny = stiff_ref.shape
+    nx, ny = (body_ref.shape[0] - 16) // 2, body_ref.shape[1]
     ext_x = nx + 2 * HALO
     field_out[0:HALO, :] = above_ref[0:HALO, :]
-    field_out[HALO:HALO + nx, :] = field_ref[0]
+    field_out[HALO:HALO + nx, :] = body_ref[0:nx, :]
     field_out[HALO + nx:ext_x, :] = below_ref[0:HALO, :]
     stiff_out[0:HALO, :] = above_ref[HALO:2 * HALO, :]
-    stiff_out[HALO:HALO + nx, :] = stiff_ref[...]
+    stiff_out[HALO:HALO + nx, :] = body_ref[nx:2 * nx, :]
     stiff_out[HALO + nx:ext_x, :] = below_ref[HALO:2 * HALO, :]
     lane = lax.broadcasted_iota(jnp.int32, (8, ny), 1)
     after = pltpu.roll(below_ref[8:16, :], nx + HALO, 1)
     before = pltpu.roll(above_ref[8:16, :], ny - nx + HALO, 1)
-    own = pltpu.roll(own_ref[8:16, :], HALO, 1)
+    own = pltpu.roll(body_ref[2 * nx:2 * nx + 8, :], HALO, 1)
     octets_out[...] = jnp.where(lane < HALO, before, jnp.where(lane < HALO + nx, own, after))
-    octets = sign_bytes(signs_ref[...])
+    octets = body_ref[2 * nx + 8:, :]
     field, stiff = field_out[...], stiff_out[...]
     lane = lax.broadcasted_iota(jnp.int32, field.shape, 1)
     first_ref[0:ext_x, :] = jnp.where(lane < HALO, field, pltpu.roll(stiff, HALO, 1))
@@ -327,7 +331,7 @@
             pltpu.VMEM((dirs, 2 * dirs), F32),
         ],
         compiler_params=pltpu.CompilerParams(
-            dimension_semantics=("arbitrary",), vmem_limit_bytes=61 * 2**20
+            dimension_semantics=("arbitrary",), vmem_limit_bytes=52 * 2**20
         ),
         name="responses",
     )(index, fields, stiffness)
@@ -478,7 +482,7 @@
             pltpu.VMEM(parts.shape, BF16),
             pltpu.SemaphoreType.DMA,
         ],
-        compiler_params=pltpu.CompilerParams(vmem_limit_bytes=16 * 2**20),
+        compiler_params=pltpu.CompilerParams(vmem_limit_bytes=52 * 2**20),
         name="finish",
     )(index, gram, parts)
 
@@ -490,13 +494,13 @@
     half = nx // 2
     index = lax.axis_index("dir")
     which = index.reshape(1)
-    stiffness, first, last = small(
-        pack_x_kernel, [(nx, ny), (16, ny), (16, ny)], [VMEM] * 4, "pack_x", 60
-    )(signs_x, heights, velocity, background)
+    body, first, last = small(
+        pack_x_kernel, [(2 * nx + 16, ny), (16, ny), (16, ny)], [VMEM] * 5, "pack_x", 60
+    )(signs_x, signs_y, heights, velocity, background)
     above, below = exchange(first, last, "sx")
     field, stiffness, octets, first, last = small(
-        pack_y_kernel, [(ext_x, ny), (ext_x, ny), (8, ny), (ext_x + 8, ny), (ext_x + 8, ny)], [VMEM] * 6, "pack_y"
-    )(signs_y, background, stiffness, first, above, below)
+        pack_y_kernel, [(ext_x, ny), (ext_x, ny), (8, ny), (ext_x + 8, ny), (ext_x + 8, ny)], [VMEM] * 3, "pack_y"
+    )(body, above, below)
     left, right = exchange(first, last, "sy")
     send, stiffness = small(
         pack_dir_kernel, [(shots, half + 2 * HALO + 8, ext_y), (half + 2 * HALO, ext_y)], [SMEM] + [VMEM] * 6, "pack_dir"

time: 113 us -> 109 us (0.965)
  local copies, waits for them, and re-layouts: 5.16 us -> 0.99 us
  waiting for transfers between devices: 4.65 us -> 6.76 us
    unnamed x13 -> x3, local copies, waits for them, and re-layouts: 5.07 us -> 0.9 us
    ppermute x2, waiting for transfers between devices: 0.01 us -> 3.3 us  [exchange(): after = lax.ppermute(first, axis, [(i + 1, i) for i in range(count - 1)])]
    pallas_call x1, Pallas kernels: 10.1 us -> 11.9 us  [finish(): pl.pallas_call(functools.partial(finish_kernel, n, scale), in_specs=[SMEM...]
where the time goes in v5:
time: 109 us; the launch traced here: 108 us
  blocking collectives  58.6 us (54%)
  Pallas kernels  27.7 us (25%)
  starting transfers between devices  12.1 us (11%)
  waiting for transfers between devices  6.76 us (6%)
  other arithmetic  1.22 us (1%)
    all_to_all x1, blocking collectives, shards(): lax.all_to_all(jnp.broadcast_to(row, (dirs, *row.shape[1:])), ('dir', 'sx...  22.3 us
    all_to_all x1, blocking collectives, shards(): lax.all_to_all(strip.reshape(PROBES, dirs // 128, 128), ('sx', 'sy'), 0, 0)  21.1 us
    all_to_all x1, blocking collectives, shards(): fields = lax.all_to_all(send, 'dir', 0, 0)  15.2 us
    pallas_call x1, Pallas kernels, responses(): pl.pallas_call(functools.partial(response_kernel, shots, nx, ny), grid=(e...  14.2 us
    pallas_call x1, Pallas kernels, finish(): pl.pallas_call(functools.partial(finish_kernel, n, scale), in_specs=[SMEM...  11.9 us
    ppermute x2, starting transfers between devices, exchange(): before = lax.ppermute(last, axis, [(i, i + 1) for i in range(count - 1)])  8.19 us
    ppermute x2, waiting for transfers between devices, exchange(): after = lax.ppermute(first, axis, [(i + 1, i) for i in range(count - 1)])  3.3 us
    ppermute x2, starting transfers between devices, exchange(): after = lax.ppermute(first, axis, [(i + 1, i) for i in range(count - 1)])  2.58 us
  transfers between devices with their start and end apart: 6, of which 4 were waited for; matrix products, arithmetic and copies ran while one was open for 0% of the time, Pallas kernels for 0%

profile of v5, /device:TPU:1, one launch (start us, length us, event | category | flops | bytes accessed | tf_op | source)
XLA Modules:
  0.0 108.1 jit_solution(13736154555674585649)
XLA Ops:
  0.6 1.5 %pack_x.1 = (f32[144,128]{1,0:T(8,128)}, f32[16,128]{1,0:T(8,128)}, f32[16,128]{1,0:T(8,128)}) custom-call(s32[1,64]{1,0:T(1,128)} %signs_ref.1, s32[1,128]{1,0:T(1,128)} %other_signs_ref.1, s32[64,128]{1,0:T(8,128)} %heights_ref.1, f32[64,128]{1,0:T(8,128)} %velocity_ref.1, f32[1,64,128]{2,1,0:T(8,128)} %field_ref.1), custom_call_target="tpu_custom_call" | custom-call | tf_op jit(solution)/shard_map/pack_x/pallas_call | solution.py:497
  2.1 4.0 %collective-permute-start = (f32[16,128]{1,0:T(8,128)}, f32[16,128]{1,0:T(8,128)S(1)}, u32[]{:S(2)}, u32[]{:S(2)}) collective-permute-start(f32[16,128]{1,0:T(8,128)} %get-tuple-element.19), channel_id=1, source_target_pairs={{0,8},{8,16},{16,24},{1,9},{9,17},{17,25},{2,10},{10,18},{18,26},{... | collective-permute-start | bytes 24584 | tf_op jit(solution)/shard_map/ppermute | solution.py:124
  6.1 1.3 %collective-permute-start.1 = (f32[16,128]{1,0:T(8,128)}, f32[16,128]{1,0:T(8,128)S(1)}, u32[]{:S(2)}, u32[]{:S(2)}) collective-permute-start(f32[16,128]{1,0:T(8,128)} %get-tuple-element.20), channel_id=1, source_target_pairs={{8,0},{16,8},{24,16},{9,1},{17,9},{25,17},{10,2},{18,10},{26,18},{... | collective-permute-start | bytes 24584 | tf_op jit(solution)/shard_map/ppermute | solution.py:125
  7.4 0.0 collective-permute-done.above_ref
  7.4 3.3 %collective-permute-done.1.below_ref = f32[16,128]{1,0:T(8,128)S(1)} collective-permute-done((f32[16,128]{1,0:T(8,128)}, f32[16,128]{1,0:T(8,128)S(1)}, u32[]{:S(2)}, u32[]{:S(2)}) %collective-permute-start.1) | collective-permute-done | bytes 8224 | tf_op jit(solution)/shard_map/ppermute | solution.py:125
  10.7 0.9 copy-done
  11.6 0.1 pack_y.1
  11.7 1.3 %collective-permute-start.3 = (f32[80,128]{1,0:T(8,128)S(1)}, f32[80,128]{1,0:T(8,128)S(1)}, u32[]{:S(2)}, u32[]{:S(2)}) collective-permute-start(f32[80,128]{1,0:T(8,128)S(1)} %get-tuple-element.24.own_ref), channel_id=1, source_target_pairs={{1,0},{2,1},{3,2},{4,3},{5,4},{6,5},{7,6},{9,8},{10,9},{11,10},{12... | collective-permute-start | bytes 122888 | tf_op jit(solution)/shard_map/ppermute | solution.py:125
  13.0 4.2 %collective-permute-start.2 = (f32[80,128]{1,0:T(8,128)S(1)}, f32[80,128]{1,0:T(8,128)S(1)}, u32[]{:S(2)}, u32[]{:S(2)}) collective-permute-start(f32[80,128]{1,0:T(8,128)S(1)} %get-tuple-element.25), channel_id=1, source_target_pairs={{0,1},{1,2},{2,3},{3,4},{4,5},{5,6},{6,7},{8,9},{9,10},{10,11},{11... | collective-permute-start | bytes 122888 | tf_op jit(solution)/shard_map/ppermute | solution.py:124
  17.2 0.0 collective-permute-done.3.right_ref
  17.2 1.1 collective-permute-done.2.left_ref
  18.3 0.1 pack_dir.1
  18.4 15.2 %all_to_all.15.field_ref = f32[8,48,136]{2,1,0:T(8,128)S(1)} all-to-all(f32[8,48,136]{2,1,0:T(8,128)S(1)} %get-tuple-element.26), channel_id=1, replica_groups=mesh['dir'=8,'sx'=4,'sy'=8] {'dir'}, dimensions={0} | all-to-all | bytes 417792 | tf_op jit(solution)/shard_map/all_to_all | solution.py:508
  33.6 14.2 %responses.1 = (f32[32,256]{1,0:T(8,128)S(1)}, f32[32,256]{1,0:T(8,128)S(1)}, bf16[32,128,512]{2,1,0:T(8,128)(2,1)}) custom-call(s32[1]{0:T(128)} %bitcast.index_ref, f32[8,48,136]{2,1,0:T(8,128)S(1)} %all_to_all.15.field_ref, f32[40,136]{1,0:T(8,128)S(1)} %get-tuple-element.27.stiff_ref), custom_call_target="tpu_custom_call" | custom-call | tf_op jit(solution)/shard_map/responses/pallas_call | solution.py:311
  47.8 0.9 collective-permute-start.4
  48.7 0.9 collective-permute-done.4
  49.5 21.1 %all_to_all.16 = f32[32,2,128]{2,1,0:T(2,128)S(1)} all-to-all(f32[32,2,128]{2,1,0:T(2,128)S(1)} %reshape.15), channel_id=1, replica_groups=mesh['dir'=8,'sx'=4,'sy'=8] {'sx','sy'}, dimensions={0} | all-to-all | bytes 65536 | tf_op jit(solution)/shard_map/all_to_all | solution.py:513
  70.7 0.1 broadcast_in_dim.2
  70.8 22.3 %all_to_all.17 = f32[256,2,128]{2,1,0:T(2,128)S(1)} all-to-all(f32[256,2,128]{2,1,0:T(2,128)S(1)} %broadcast_in_dim.2), channel_id=1, replica_groups=mesh['dir'=8,'sx'=4,'sy'=8] {'dir','sx','sy'}, dimensions={0} | all-to-all | bytes 524288 | tf_op jit(solution)/shard_map/all_to_all | solution.py:515
  93.1 11.9 %finish.1 = (f32[32,256]{1,0:T(8,128)}, f32[32,32,128]{2,1,0:T(8,128)S(1)}, f32[32,32,128]{2,1,0:T(8,128)S(1)}) custom-call(s32[1]{0:T(128)} %bitcast.index_ref, f32[256,256]{1,0:T(8,128)S(1)} %bitcast.5, bf16[32,128,512]{2,1,0:T(8,128)(2,1)} %get-tuple-element.30.parts_any), custom_call_target="tpu_custom_call" | custom-call | tf_op jit(solution)/shard_map/finish/pallas_call | solution.py:471
  104.9 0.5 collective-permute-start.5
  105.4 1.5 %collective-permute-done.5 = f32[32,32,128]{2,1,0:T(8,128)S(1)} collective-permute-done((f32[32,32,128]{2,1,0:T(8,128)S(1)}, f32[32,32,128]{2,1,0:T(8,128)S(1)}, u32[]{:S(2)}, u32[]{:S(2)}) %collective-permute-start.5) | collective-permute-done | bytes 524320 | tf_op jit(solution)/shard_map/ppermute | solution.py:519
  106.9 0.1 broadcast_select_fusion.1
  107.1 1.1 pad_maximum_fusion
  (5 shorter events, 0.1 us)
Async XLA Ops:
  2.1 5.3 %collective-permute-start = (f32[16,128]{1,0:T(8,128)}, f32[16,128]{1,0:T(8,128)S(1)}, u32[]{:S(2)}, u32[]{:S(2)}) collective-permute-start(f32[16,128]{1,0:T(8,128)} %get-tuple-element.19), channel_id=1, source_target_pairs={{0,8},{8,16},{16,24},{1,9},{9,17},{17,25},{2,10},{10,18},{18,26},{... | collective-permute-start | bytes 24584 | tf_op jit(solution)/shard_map/ppermute | solution.py:124
  6.1 4.6 %collective-permute-start.1 = (f32[16,128]{1,0:T(8,128)}, f32[16,128]{1,0:T(8,128)S(1)}, u32[]{:S(2)}, u32[]{:S(2)}) collective-permute-start(f32[16,128]{1,0:T(8,128)} %get-tuple-element.20), channel_id=1, source_target_pairs={{8,0},{16,8},{24,16},{9,1},{17,9},{25,17},{10,2},{18,10},{26,18},{... | collective-permute-start | bytes 24584 | tf_op jit(solution)/shard_map/ppermute | solution.py:125
  10.7 0.9 copy-start
  11.7 5.5 %collective-permute-start.3 = (f32[80,128]{1,0:T(8,128)S(1)}, f32[80,128]{1,0:T(8,128)S(1)}, u32[]{:S(2)}, u32[]{:S(2)}) collective-permute-start(f32[80,128]{1,0:T(8,128)S(1)} %get-tuple-element.24.own_ref), channel_id=1, source_target_pairs={{1,0},{2,1},{3,2},{4,3},{5,4},{6,5},{7,6},{9,8},{10,9},{11,10},{12... | collective-permute-start | bytes 122888 | tf_op jit(solution)/shard_map/ppermute | solution.py:125
  13.0 5.3 %collective-permute-start.2 = (f32[80,128]{1,0:T(8,128)S(1)}, f32[80,128]{1,0:T(8,128)S(1)}, u32[]{:S(2)}, u32[]{:S(2)}) collective-permute-start(f32[80,128]{1,0:T(8,128)S(1)} %get-tuple-element.25), channel_id=1, source_target_pairs={{0,1},{1,2},{2,3},{3,4},{4,5},{5,6},{6,7},{8,9},{9,10},{10,11},{11... | collective-permute-start | bytes 122888 | tf_op jit(solution)/shard_map/ppermute | solution.py:124
  47.8 1.7 %collective-permute-start.4 = (f32[32,256]{1,0:T(8,128)S(1)}, f32[32,256]{1,0:T(8,128)S(1)}, u32[]{:S(2)}, u32[]{:S(2)}) collective-permute-start(f32[32,256]{1,0:T(8,128)S(1)} %get-tuple-element.29), channel_id=1, source_target_pairs={{0,32},{32,0},{64,96},{96,64},{128,160},{160,128},{192,224},{224,1... | collective-permute-start | bytes 98312 | tf_op jit(solution)/shard_map/ppermute | solution.py:512
  104.9 2.0 %collective-permute-start.5 = (f32[32,32,128]{2,1,0:T(8,128)S(1)}, f32[32,32,128]{2,1,0:T(8,128)S(1)}, u32[]{:S(2)}, u32[]{:S(2)}) collective-permute-start(f32[32,32,128]{2,1,0:T(8,128)S(1)} %get-tuple-element.31), channel_id=1, source_target_pairs={{0,32},{32,0},{64,96},{96,64},{128,160},{160,128},{192,224},{224,1... | collective-permute-start | bytes 1572872 | tf_op jit(solution)/shard_map/ppermute | solution.py:519
